TPU v7x, 256 devices: a whole 4x4x8 slice. The times are simulated.
256 devices in a mesh: section: 4 (over y), expert: 8 (over z_hi, core), dp: 8 (over z_lo, x).
Axes of the slice: x: 4, y: 4, z: 8 (z_hi: 4, z_lo: 2; z = z_hi * 2 + z_lo), core: 2. Of those that a mesh axis runs over, the one named last changes fastest.
Arguments:
- layer_input: bfloat16 [4096, 2048], P(('section', 'expert')), may hold values from -6 to 6
- out_grad: bfloat16 [4096, 2048], P(('section', 'expert')), may hold values from -6 to 6
- expert_ids: int32 [4096, 2], P(('section', 'expert')), may hold values from 0 to 3, all different within a row; in each aligned block of 128 rows (0 to 127, 128 to 255, ...) at most 80 rows name the same one
- gate_weights: bfloat16 [4096, 2], P(('section', 'expert')), may hold values from 0.01 to 0.99, as said below
- w_gate: bfloat16 [4, 32768, 2048], P('section', ('expert', 'dp')), may hold values from -0.125 to 0.125
- w_up: bfloat16 [4, 32768, 2048], P('section', ('expert', 'dp')), may hold values from -0.125 to 0.125
- w_down: bfloat16 [4, 32768, 2048], P('section', ('expert', 'dp')), may hold values from -0.0625 to 0.0625
Outputs:
- prev_grad: bfloat16 [4096, 2048], P(('section', 'expert'))
- router_grad: float32 [4096, 2], P(('section', 'expert'))
- grad_gate: bfloat16 [4, 32768, 2048], P('section', ('expert', 'dp'))
- grad_up: bfloat16 [4, 32768, 2048], P('section', ('expert', 'dp'))
- grad_down: bfloat16 [4, 32768, 2048], P('section', ('expert', 'dp'))
Inputs may be any that keep to these rules, and one draw needn't show every extreme that they name: `expert_ids`: A token names 2 different experts. In each aligned block of 128 rows (the tokens of one device) no expert is named by more than 80 tokens. `gate_weights`: A token's two gate weights sum to one up to rounding; the first is no smaller than the second.
All inputs are finite; a program needn't handle non-finite values.
Results may differ from a plain program's by a relative error of at most 0.0049.
Values may be sent and summed in bfloat16 or wider, within the bound.
No kernel may reach another device: no remote copies, remote signals or barrier semaphores. Data moves between devices by JAX's collectives and lax.ppermute only.
A program may use at most 128 MiB of HBM per device.

v0:
```python
import functools

import jax
import jax.numpy as jnp
from jax import lax
from jax.experimental import pallas as pl
from jax.experimental.pallas import tpu as pltpu
from jax.sharding import PartitionSpec as P

EXPERTS = 4
CAP = 80
TOK = 128
D = 2048
UNITS = 512
ROWS = 640
PAIR = 2 * CAP
AWAY = ROWS - PAIR
HOT = 2 * EXPERTS * CAP
BF = jnp.bfloat16
F32 = jnp.float32
MIB = 1 << 20


def cost(flops, moved):
    return pl.CostEstimate(flops=flops, bytes_accessed=moved, transcendentals=0)


def core_swap(a):
    return lax.ppermute(a, "expert", [(i, i ^ 1) for i in range(8)])


def chip_shift(a, r):
    if r != 2:
        return lax.ppermute(a, "expert", [(i, (i + 2 * r) % 8) for i in range(8)])
    route = [(e * 8 + d, (e + 4) % 8 * 8 + (d + 4) % 8) for e in range(8) for d in range(8)]
    return lax.ppermute(a, ("expert", "dp"), route)


def chip_return(a, r):
    route = []
    for s in range(4):
        for e in range(8):
            for d in range(8):
                to = ((s - 1) % 4 * 8 + (e - 2 * r) % 8) * 8 + (d + (4 if r == 2 else 0)) % 8
                route.append(((s * 8 + e) * 8 + d, to))
    return lax.ppermute(a, ("section", "expert", "dp"), route)


def x_shift(a, j):
    return lax.ppermute(a, "dp", [(i, i // 4 * 4 + (i + j) % 4) for i in range(8)])


def pair_swap(a):
    return lax.ppermute(a, "dp", [(i, (i + 4) % 8) for i in range(8)])


def section_shift(a, by):
    return lax.ppermute(a, "section", [(s, (s + by) % 4) for s in range(4)])


def next_section_pair(a):
    route = [(s * 8 + d, (s + 1) % 4 * 8 + (d + 4) % 8) for s in range(4) for d in range(8)]
    return lax.ppermute(a, ("section", "dp"), route)


def dot(a, b, dims):
    return lax.dot_general(a, b, (dims, ((), ())), preferred_element_type=F32)


def place_rows(meta):
    earlier = lax.broadcasted_iota(jnp.int32, (TOK, TOK), 0)
    later = lax.broadcasted_iota(jnp.int32, (TOK, TOK), 1)
    upto = (earlier <= later).astype(F32).astype(BF)
    return dot(meta, upto, ((1,), (0,))) - 1.0


def hot_rows(named, place, r):
    slot = lax.broadcasted_iota(jnp.int32, (TOK, TOK), 0).astype(F32)
    hit = (slot == place[r : r + 1]) & (named[r : r + 1] > 0.5)
    return hit.astype(F32).astype(BF)


def slots_kernel(where_ref, mine_ref, got_ref, *outs):
    sends, gate0, pack = outs[:3], outs[3], outs[4]
    core = where_ref[1]
    row = lax.broadcasted_iota(jnp.int32, (16, TOK), 0)
    gate_rows = []
    for c in range(2):
        block = jnp.where(core == c, mine_ref[...].astype(F32), got_ref[...].astype(F32)).astype(BF)
        tokens = block[:TOK]
        meta = block[TOK : TOK + 16, :TOK]
        named = meta.astype(F32)
        place = place_rows(meta)
        for h in range(2):
            at = HOT + (2 * c + h) * TOK
            pack[at : at + TOK, :] = tokens[:, 256 + h * TOK : 384 + h * TOK]
        for r in range(EXPERTS):
            hot = hot_rows(named, place, r)
            at = (c * EXPERTS + r) * CAP
            pack[at : at + CAP, :] = hot[:CAP]
            if r > 0:
                filled = dot(hot[:CAP], tokens, ((1,), (0,))).astype(BF)
                sends[r - 1][c * CAP : (c + 1) * CAP, :] = filled[:, :256]
                sends[r - 1][PAIR + c * CAP : PAIR + (c + 1) * CAP, :] = filled[:, 256:]
            gates = dot(meta, hot, ((1,), (1,)))
            gate_rows.append(gates[4 + r : 5 + r])
    for r in range(EXPERTS):
        tile = jnp.where(row == 0, gate_rows[r], jnp.where(row == 1, gate_rows[4 + r], 0.0))
        if r == 0:
            gate0[...] = tile.astype(BF)
        else:
            sends[r - 1][2 * PAIR :, :TOK] = tile.astype(BF)
            sends[r - 1][2 * PAIR :, TOK:] = jnp.zeros((16, TOK), BF)


BLOCK = pl.BlockSpec()
VMEM = pl.BlockSpec(memory_space=pltpu.VMEM)
ANY = pl.BlockSpec(memory_space=pltpu.HBM)
SMEM = pl.BlockSpec(memory_space=pltpu.SMEM)


def params(mib):
    return pltpu.CompilerParams(vmem_limit_bytes=mib * MIB)


def fill_slots(where, mine, got):
    shapes = (
        [jax.ShapeDtypeStruct((2 * PAIR + 16, 256), BF)] * 3
        + [
            jax.ShapeDtypeStruct((16, TOK), BF),
            jax.ShapeDtypeStruct((HOT + 4 * TOK, TOK), BF),
        ]
    )
    return pl.pallas_call(
        slots_kernel,
        out_shape=shapes,
        in_specs=[SMEM] + [BLOCK] * 2,
        out_specs=[BLOCK] * 5,
        compiler_params=params(8),
        cost_estimate=cost(100_000_000, 2_000_000),
        name="fill_slots",
    )(where, mine, got)


def local_kernel(mine_ref, input_ref, grad_ref, out_ref):
    meta = mine_ref[TOK : TOK + 16, :TOK]
    hot = hot_rows(meta.astype(F32), place_rows(meta), 0)[:CAP]
    for at, source in enumerate((input_ref, grad_ref)):
        for part in range(4):
            columns = slice(part * 512, part * 512 + 512)
            out_ref[at, :, columns] = dot(hot, source[:, columns], ((1,), (0,))).astype(BF)


def local_slots(mine, layer_input, out_grad):
    return pl.pallas_call(
        local_kernel,
        out_shape=pltpu.HBM((2, CAP, D), BF),
        in_specs=[BLOCK] * 3,
        out_specs=BLOCK,
        compiler_params=params(8),
        cost_estimate=cost(100_000_000, 2_000_000),
        name="local_slots",
    )(mine, pinned(layer_input), pinned(out_grad))


def column(where_ref, j, flip):
    x, core = where_ref[0], where_ref[1]
    half = core if flip == 0 else 1 - core
    return pl.multiple_of(lax.rem(x + j, 4) * 512 + half * 256, 256)


def copy_all(pairs, sems, first=0):
    copies = [
        pltpu.make_async_copy(source, target, sems.at[first + at])
        for at, (source, target) in enumerate(pairs)
    ]
    for c in copies:
        c.start()
    return copies


def wait_all(copies):
    for c in copies:
        c.wait()


def gather_rows(where_ref, pieces, local, which, whole):
    core = where_ref[1]
    pairs = []
    for flip in range(2):
        half = core if flip == 0 else 1 - core
        rows = pl.ds(pl.multiple_of(half * CAP, 16), CAP)
        pairs.append((local[flip].at[which], whole.at[rows, :]))
        for j, piece in enumerate(pieces[4 * flip : 4 * flip + 4]):
            columns = pl.ds(column(where_ref, (4 - j) % 4, flip), 256)
            rows = slice(which * AWAY, which * AWAY + AWAY)
            pairs.append((piece.at[rows, :], whole.at[PAIR:, columns]))
    return pairs


def expert_kernel(where_ref, *refs):
    pieces, local = refs[:8], refs[8:10]
    gate_rows, up_rows, down_rows, gates_ref = refs[10:14]
    input_out, grad_out, gpg_out, upg_out, scaled_out, router, grads = refs[14:21]
    inputs, out_grads, scaled, sems = refs[21:]
    loads = copy_all(
        gather_rows(where_ref, pieces, local, 0, inputs)
        + gather_rows(where_ref, pieces, local, 1, out_grads),
        sems,
    )
    wait_all(loads[:10])
    stores = copy_all([(inputs, input_out)], sems, 20)
    gates = gates_ref[...]
    router_sum = jnp.zeros((ROWS, 1), F32)
    for n in range(2):
        units = slice(n * 256, n * 256 + 256)
        ups = slice(UNITS + n * 256, UNITS + n * 256 + 256)
        v = dot(inputs[...], gate_rows[units, :], ((1,), (1,)))
        up = dot(inputs[...], up_rows[units, :], ((1,), (1,)))
        if n == 0:
            wait_all(loads[10:])
            stores += copy_all([(out_grads, grad_out)], sems, 21)
        hidden_grad = dot(out_grads[...], down_rows[units, :], ((1,), (1,)))
        s = jax.nn.sigmoid(v)
        activated = v * s
        hidden = activated * up
        router_sum = router_sum + jnp.sum(hidden * hidden_grad, axis=1, keepdims=True)
        scaled_grad = gates * hidden_grad
        grads[:, units] = (scaled_grad * up * (s * (1.0 + v * (1.0 - s)))).astype(BF)
        grads[:, ups] = (scaled_grad * activated).astype(BF)
        scaled[:, units] = (gates * hidden).astype(BF)
        stores += copy_all(
            [
                (grads.at[:, units], gpg_out.at[:, units]),
                (grads.at[:, ups], upg_out.at[:, units]),
                (scaled.at[:, units], scaled_out.at[:, units]),
            ],
            sems,
            22 + 3 * n,
        )
    router[...] = router_sum
    wait_all(stores)


def expert_work(where, pieces, local, w_gate, w_up, w_down, gates):
    return pl.pallas_call(
        expert_kernel,
        out_shape=[
            pltpu.HBM((ROWS, D), BF),
            pltpu.HBM((ROWS, D), BF),
            pltpu.HBM((ROWS, UNITS), BF),
            pltpu.HBM((ROWS, UNITS), BF),
            pltpu.HBM((ROWS, UNITS), BF),
            jax.ShapeDtypeStruct((ROWS, 1), F32),
            jax.ShapeDtypeStruct((ROWS, 2 * UNITS), BF),
        ],
        in_specs=[SMEM] + [ANY] * 10 + [VMEM] * 4,
        out_specs=[ANY] * 5 + [VMEM] * 2,
        scratch_shapes=[
            pltpu.VMEM((ROWS, D), BF),
            pltpu.VMEM((ROWS, D), BF),
            pltpu.VMEM((ROWS, UNITS), BF),
            pltpu.SemaphoreType.DMA((28,)),
        ],
        compiler_params=params(16),
        cost_estimate=cost(3 * 2 * ROWS * D * UNITS, 12_000_000),
        name="expert_work",
    )(where, *map(pinned, pieces), *map(pinned, local), w_gate, w_up, w_down, gates)


CHUNKS = ((2, 1), (3, 0))


def arrange_kernel(where_ref, gate_ref, up_ref, *refs):
    outs, (held, sems) = refs[:4], refs[4:]
    pairs = []
    for n in range(4):
        chunks = CHUNKS[n % 2]
        for h, j in enumerate(chunks):
            columns = pl.ds(column(where_ref, j, n // 2), 256)
            for at, source in enumerate((gate_ref, up_ref)):
                rows = slice(at * UNITS, (at + 1) * UNITS)
                target = held.at[n, h, rows, :]
                pairs.append((source.at[:, columns], target))
    loads = copy_all(pairs, sems)
    stores = []
    for n in range(4):
        wait_all(loads[4 * n : 4 * n + 4])
        stores += copy_all([(held.at[n], outs[n])], sems, 16 + n)
    wait_all(stores)


def arrange_weights(where, w_gate, w_up):
    return pl.pallas_call(
        arrange_kernel,
        out_shape=[pltpu.HBM((2, 2 * UNITS, 256), BF)] * 4,
        in_specs=[SMEM] + [ANY] * 2,
        out_specs=[ANY] * 4,
        scratch_shapes=[
            pltpu.VMEM((4, 2, 2 * UNITS, 256), BF),
            pltpu.SemaphoreType.DMA((20,)),
        ],
        compiler_params=params(8),
        cost_estimate=cost(0, 8_000_000),
        name="arrange_weights",
    )(where, w_gate, w_up)


def part_kernel(chunks, grads, got, own, given, router_a, router_b, *outs):
    tail = hi_lo(router_a[...] + router_b[...])
    for n, (j, out) in enumerate(zip(chunks, outs)):
        total = dot(grads[...], own[n], ((1,), (0,)))
        total = total + dot(got[...], given[n], ((1,), (0,)))
        if j == 0:
            out[...] = total
        else:
            out[:ROWS, :] = total.astype(BF)
            out[ROWS:, :TOK] = tail
            out[ROWS:, TOK:] = jnp.zeros((16, TOK), BF)


def part_work(chunks, grads, got, own, given, router_a, router_b):
    shapes = [
        jax.ShapeDtypeStruct((ROWS, 256), F32)
        if j == 0
        else jax.ShapeDtypeStruct((ROWS + 16, 256), BF)
        for j in chunks
    ]
    return pl.pallas_call(
        functools.partial(part_kernel, chunks),
        out_shape=shapes,
        in_specs=[VMEM] * 6,
        out_specs=[VMEM] * 2,
        compiler_params=params(8),
        cost_estimate=cost(2 * ROWS * 4 * UNITS * 512, 6_000_000),
        name="part_work",
    )(grads, got, own, given, router_a, router_b)


def hi_lo(value):
    high = value.astype(BF)
    return jnp.concatenate([high.astype(F32), value - high.astype(F32)]).astype(BF)


def x_sum_kernel(where_ref, keep, router_a, router_b, *refs):
    arrived, outs = refs[:3], refs[3:]
    x = where_ref[0]
    own = hi_lo(router_a[...] + router_b[...]).astype(F32)
    tails = [own] + [a[ROWS:, :TOK].astype(F32) for a in arrived]
    tails = [t[:8] + t[8:] for t in tails]
    total = jnp.zeros((8, TOK), F32)
    for at in range(4):
        j = lax.rem(x - at + 4, 4)
        picked = tails[3]
        for k in range(3):
            picked = jnp.where(j == k, tails[k], picked)
        total = total + picked
    tail = hi_lo(total)
    for r in range(EXPERTS):
        rows = slice(r * PAIR, r * PAIR + PAIR)
        block = keep[rows, :]
        for a in arrived:
            block = block + a[rows, :].astype(F32)
        outs[r][:PAIR, :] = block.astype(BF)
        outs[r][PAIR:, :TOK] = tail
        outs[r][PAIR:, TOK:] = jnp.zeros((16, TOK), BF)


def x_sum(where, keep, router_a, router_b, arrived):
    return pl.pallas_call(
        x_sum_kernel,
        out_shape=[jax.ShapeDtypeStruct((PAIR + 16, 256), BF)] * 4,
        in_specs=[SMEM] + [VMEM] * 6,
        out_specs=[BLOCK] * 4,
        compiler_params=params(8),
        cost_estimate=cost(1_000_000, 3_000_000),
        name="x_sum",
    )(where, keep, router_a, router_b, *arrived)


def return_kernel(*refs):
    parts, (pack, out_ref, router_ref) = refs[:4], refs[4:]
    row = lax.broadcasted_iota(jnp.int32, (8, TOK), 0)
    router = jnp.zeros((8, TOK), F32)
    for c in range(2):
        total = jnp.zeros((TOK, 256), F32)
        for r in range(EXPERTS):
            at = (c * EXPERTS + r) * CAP
            hot = pack[at : at + CAP, :]
            total += dot(hot, parts[r][c * CAP : (c + 1) * CAP, :], ((0,), (0,)))
            tail = dot(parts[r][PAIR : PAIR + 16, :CAP], hot, ((1,), (0,)))
            at = 2 * r + c
            value = tail[at : at + 1] + tail[8 + at : 9 + at]
            router = jnp.where(row == 4 * c + r, value, router)
        out_ref[c * TOK : (c + 1) * TOK, :] = total.astype(BF)
    router_ref[...] = router


def return_slots(parts, pack):
    return pl.pallas_call(
        return_kernel,
        out_shape=[
            jax.ShapeDtypeStruct((2 * TOK, 256), BF),
            jax.ShapeDtypeStruct((8, TOK), F32),
        ],
        in_specs=[BLOCK] * 5,
        out_specs=[BLOCK] * 2,
        compiler_params=params(8),
        cost_estimate=cost(100_000_000, 1_500_000),
        name="return_slots",
    )(*parts, pack)


def final_kernel(where_ref, partial, got, pack, stays, goes):
    core = where_ref[1]
    total = partial[...].astype(F32) + got[...].astype(F32)
    final = []
    for c in range(2):
        for h in range(2):
            at = HOT + (2 * c + h) * TOK
            columns = slice(h * TOK, h * TOK + TOK)
            rows = total[c * TOK : (c + 1) * TOK, columns]
            final.append(rows + pack[at : at + TOK, :].astype(F32))
    for h in range(2):
        columns = slice(h * TOK, h * TOK + TOK)
        stays[:, columns] = jnp.where(core == 0, final[h], final[2 + h]).astype(BF)
        goes[:, columns] = jnp.where(core == 0, final[2 + h], final[h]).astype(BF)


def finish(where, partial, got, pack):
    return pl.pallas_call(
        final_kernel,
        out_shape=[
            jax.ShapeDtypeStruct((TOK, 256), BF),
            jax.ShapeDtypeStruct((TOK, 256), BF),
        ],
        in_specs=[SMEM] + [BLOCK] * 3,
        out_specs=[BLOCK] * 2,
        compiler_params=params(8),
        cost_estimate=cost(1_000_000, 600_000),
        name="finish",
    )(where, partial, got, pack)


def x_gather(own):
    return [own] + [x_shift(own, j) for j in (1, 2, 3)]


def weight_grad(a, b):
    return dot(a, b, ((0,), (0,))).astype(BF)[None]


def pinned(a):
    return pltpu.with_memory_space_constraint(a, pltpu.HBM)


def on_device(layer_input, out_grad, expert_ids, gate_weights, w_gate, w_up, w_down):
    spot = lax.axis_index("expert")
    chip, core = spot // 2, spot % 2
    x = lax.axis_index("dp") % 4
    where = jnp.stack([x, core]).astype(jnp.int32)
    gate_rows, up_rows = pinned(w_gate[0]), pinned(w_up[0])

    relative = (expert_ids - chip) & 3
    picked = relative.T[None] == jnp.arange(EXPERTS, dtype=jnp.int32)[:, None, None]
    named = jnp.sum(picked.astype(F32), axis=1)
    weight = jnp.sum(jnp.where(picked, gate_weights.T.astype(F32)[None], 0.0), axis=1)
    meta = jnp.pad(jnp.concatenate([named, weight]).astype(BF), ((0, 8), (0, 384)))

    def own_columns(half):
        start = x * 512 + half * 256
        a = lax.dynamic_slice(layer_input, (0, start), (TOK, 256))
        b = lax.dynamic_slice(out_grad, (0, start), (TOK, 256))
        return jnp.concatenate([jnp.concatenate([a, b], axis=1), meta], axis=0)

    mine = own_columns(core)
    got = core_swap(own_columns(1 - core))
    filled = fill_slots(where, mine, got)
    gate0, pack = filled[3:]
    away = {r: chip_shift(filled[r - 1], r) for r in (2, 1, 3)}
    away = [away[r] for r in (1, 2, 3)]
    own_a, own_b, give_a, give_b = arrange_weights(where, gate_rows, up_rows)
    local = local_slots(mine, layer_input, out_grad)
    away, given, local = lax.optimization_barrier((away, [give_a, give_b], local))
    local = [local, core_swap(local)]
    rows = [z[:PAIR] for z in away] + [z[PAIR : 2 * PAIR] for z in away]
    pieces = x_gather(jnp.concatenate(rows))
    own, near, given, pack = lax.optimization_barrier((pieces[0], pieces[1], given, pack))
    pack = section_shift(pack, -1)
    given = [pinned(core_swap(g)) for g in given]
    pieces[:2] = own, near
    gates = jnp.stack([gate0[:2, :CAP]] + [z[2 * PAIR : 2 * PAIR + 2, :CAP] for z in away])
    gates = gates.astype(F32).reshape(ROWS, 1)
    pieces = pieces + [core_swap(p) for p in pieces]
    pieces, given, pack = lax.optimization_barrier((pieces, given, pack))

    rows_input, rows_grad, gpg, upg, scaled, router, half = expert_work(
        where, pieces, local, w_gate[0], w_up[0], w_down[0], gates
    )
    got = core_swap(half)
    router = jnp.pad(router.reshape(8, CAP), ((0, 0), (0, TOK - CAP)))
    routers = (router, core_swap(router))
    far, near = part_work(CHUNKS[0], half, got, own_a, given[0], *routers)
    far, near = x_shift(far, 2), x_shift(near, 1)
    back, keep = part_work(CHUNKS[1], half, got, own_b, given[1], *routers)
    gpg, upg, scaled, keep = lax.optimization_barrier((gpg, upg, scaled, keep))
    arrived = [near, far, x_shift(back, 3)]
    grads = [weight_grad(gpg, rows_input), weight_grad(upg, rows_input)]
    keep, grads = lax.optimization_barrier((keep, grads))
    blocks = x_sum(where, keep, *routers, arrived)
    blocks, scaled = lax.optimization_barrier((blocks, scaled))
    blocks = [chip_return(blocks[r], r) for r in range(EXPERTS)]
    grads.append(weight_grad(scaled, rows_grad))
    blocks, grads = lax.optimization_barrier((blocks, grads))

    partial, by_expert = return_slots(blocks, pack)
    by_expert = section_shift(by_expert, 1) + next_section_pair(by_expert)
    stays, goes = finish(where, partial, pair_swap(partial), pack)
    goes, by_expert = lax.optimization_barrier((goes, by_expert))
    goes = core_swap(goes)
    low = jnp.where(core == 0, stays, goes)
    high = jnp.where(core == 0, goes, stays)
    block = jnp.concatenate([low, high], axis=1)
    prev_grad = jnp.zeros((TOK, D), BF)
    pieces = [block] + [x_shift(block, j) for j in (1, 2, 3)]
    for j, piece in enumerate(pieces):
        prev_grad = lax.dynamic_update_slice(prev_grad, piece, (0, (x - j) % 4 * 512))
    by_expert = jnp.where(core == 0, by_expert[:4], by_expert[4:])
    router_grad = jnp.sum(jnp.where(picked, by_expert[:, None, :], 0.0), axis=0).T
    return (prev_grad, router_grad, *grads)


def solution(mesh):
    tokens = P(("section", "expert"), None)
    units = P("section", ("expert", "dp"), None)
    return jax.shard_map(
        on_device,
        mesh=mesh,
        in_specs=(tokens, tokens, tokens, tokens, units, units, units),
        out_specs=(tokens, tokens, units, units, units),
        check_vma=False,
    )
```

profile of v0, /device:TPU:7, one launch (start us, length us, event | category | flops | bytes accessed | tf_op | source)
XLA Modules:
  0.0 142.4 jit_solution(3987898826677694224)
XLA Ops:
  6.0 3.1 %collective-permute-start.1 = (bf16[336,256]{1,0:T(8,128)(2,1)S(1)}, bf16[336,256]{1,0:T(8,128)(2,1)S(1)}, u32[]{:S(2)}, u32[]{:S(2)}) collective-permute-start(bf16[336,256]{1,0:T(8,128)(2,1)S(1)} %get-tuple-element.76), channel_id=1, source_target_pairs={{0,16},{8,24},{16,32},{24,40},{32,48},{40,56},{48,0},{56,8},{1,17}... | collective-permute-start | bytes 516104 | tf_op jit(solution)/shard_map/ppermute | solution.py:34
  9.1 4.7 %collective-permute-start.2 = (bf16[336,256]{1,0:T(8,128)(2,1)S(1)}, bf16[336,256]{1,0:T(8,128)(2,1)S(1)}, u32[]{:S(2)}, u32[]{:S(2)}) collective-permute-start(bf16[336,256]{1,0:T(8,128)(2,1)S(1)} %get-tuple-element.77), channel_id=1, source_target_pairs={{0,36},{1,37},{2,38},{3,39},{4,32},{5,33},{6,34},{7,35},{8,44},{9,... | collective-permute-start | bytes 516104 | tf_op jit(solution)/shard_map/ppermute | solution.py:36
  13.8 2.4 %collective-permute-start.3 = (bf16[336,256]{1,0:T(8,128)(2,1)S(1)}, bf16[336,256]{1,0:T(8,128)(2,1)S(1)}, u32[]{:S(2)}, u32[]{:S(2)}) collective-permute-start(bf16[336,256]{1,0:T(8,128)(2,1)S(1)} %get-tuple-element.78), channel_id=1, source_target_pairs={{0,48},{8,56},{16,0},{24,8},{32,16},{40,24},{48,32},{56,40},{1,49}... | collective-permute-start | bytes 516104 | tf_op jit(solution)/shard_map/ppermute | solution.py:34
  16.1 4.2 %arrange_weights.1 = (bf16[2,1024,256]{2,1,0:T(8,128)(2,1)}, bf16[2,1024,256]{2,1,0:T(8,128)(2,1)}, bf16[2,1024,256]{2,1,0:T(8,128)(2,1)}, bf16[2,1024,256]{2,1,0:T(8,128)(2,1)}) custom-call(s32[2]{0:T(128)S(1)} %pad_add_fusion.where_ref, bf16[512,2048]{1,0:T(8,128)(2,1)} %bitcast.30, bf16[512,2048]{1,0:T(8,128)(2,1)} %bitcast.32), custom_call_target="tpu_custom_call" | custom-call | bytes 8000000 | tf_op jit(solution)/shard_map/arrange_weights/pallas_call | solution.py:294
  20.3 2.7 %local_slots.1.refs_8_ = bf16[2,80,2048]{2,1,0:T(8,128)(2,1)} custom-call(bf16[144,512]{1,0:T(8,128)(2,1)S(1)} %get-tuple-element.158.mine_ref, bf16[128,2048]{1,0:T(8,128)(2,1)} %input_ref.1, bf16[128,2048]{1,0:T(8,128)(2,1)} %grad_ref.1), custom_call_target="tpu_custom_call" | custom-call | flops 100000000 | bytes 2000000 | tf_op jit(solution)/shard_map/local_slots/pallas_call | solution.py:155
  23.1 3.0 %collective-permute-done.2 = bf16[336,256]{1,0:T(8,128)(2,1)S(1)} collective-permute-done((bf16[336,256]{1,0:T(8,128)(2,1)S(1)}, bf16[336,256]{1,0:T(8,128)(2,1)S(1)}, u32[]{:S(2)}, u32[]{:S(2)}) %collective-permute-start.2) | collective-permute-done | bytes 172064 | tf_op jit(solution)/shard_map/ppermute | solution.py:36
  26.0 3.0 %collective-permute-done.3 = bf16[336,256]{1,0:T(8,128)(2,1)S(1)} collective-permute-done((bf16[336,256]{1,0:T(8,128)(2,1)S(1)}, bf16[336,256]{1,0:T(8,128)(2,1)S(1)}, u32[]{:S(2)}, u32[]{:S(2)}) %collective-permute-start.3) | collective-permute-done | bytes 172064 | tf_op jit(solution)/shard_map/ppermute | solution.py:34
  31.8 9.0 %collective-permute-done.4.refs_1_ = bf16[960,256]{1,0:T(8,128)(2,1)S(1)} collective-permute-done((bf16[960,256]{1,0:T(8,128)(2,1)S(1)}, bf16[960,256]{1,0:T(8,128)(2,1)S(1)}, u32[]{:S(2)}, u32[]{:S(2)}) %collective-permute-start.4) | collective-permute-done | bytes 491552 | tf_op jit(solution)/shard_map/ppermute | solution.py:50
  40.8 2.7 %collective-permute-start.13 = (bf16[1152,128]{1,0:T(8,128)(2,1)S(1)}, bf16[1152,128]{1,0:T(8,128)(2,1)S(1)}, u32[]{:S(2)}, u32[]{:S(2)}) collective-permute-start(bf16[1152,128]{1,0:T(8,128)(2,1)S(1)} %get-tuple-element.91), channel_id=1, source_target_pairs={{0,192},{64,0},{128,64},{192,128},{1,193},{65,1},{129,65},{193,129... | collective-permute-start | bytes 884744 | tf_op jit(solution)/shard_map/ppermute | solution.py:58
  43.6 4.0 %collective-permute-start.7 = (bf16[960,256]{1,0:T(8,128)(2,1)S(1)}, bf16[960,256]{1,0:T(8,128)(2,1)S(1)}, u32[]{:S(2)}, u32[]{:S(2)}) collective-permute-start(bf16[960,256]{1,0:T(8,128)(2,1)S(1)} %slice_dynamic-update-slice_fusion.refs_0_), channel_id=1, source_target_pairs={{0,8},{8,0},{16,24},{24,16},{32,40},{40,32},{48,56},{56,48},{1,9},... | collective-permute-start | bytes 1474568 | tf_op jit(solution)/shard_map/ppermute | solution.py:29
  47.6 7.3 %collective-permute-start.11 = (bf16[2,1024,256]{2,1,0:T(8,128)(2,1)}, bf16[2,1024,256]{2,1,0:T(8,128)(2,1)}, u32[]{:S(2)}, u32[]{:S(2)}) collective-permute-start(bf16[2,1024,256]{2,1,0:T(8,128)(2,1)} %get-tuple-element.89), channel_id=1, source_target_pairs={{0,8},{8,0},{16,24},{24,16},{32,40},{40,32},{48,56},{56,48},{1,9},... | collective-permute-start | bytes 3145736 | tf_op jit(solution)/shard_map/ppermute | solution.py:29
  56.6 4.0 %collective-permute-done.10.refs_7_ = bf16[960,256]{1,0:T(8,128)(2,1)} collective-permute-done((bf16[960,256]{1,0:T(8,128)(2,1)}, bf16[960,256]{1,0:T(8,128)(2,1)}, u32[]{:S(2)}, u32[]{:S(2)}) %collective-permute-start.10) | collective-permute-done | bytes 491552 | tf_op jit(solution)/shard_map/ppermute | solution.py:29
  61.4 1.6 %copy-done.1 = bf16[1,512,2048]{2,1,0:T(8,128)(2,1)S(1)} copy-done((bf16[1,512,2048]{2,1,0:T(8,128)(2,1)S(1)}, bf16[1,512,2048]{2,1,0:T(8,128)(2,1)}, u32[]{:S(2)}) %copy-start.1) | copy-done | bytes 2097176
  63.0 1.6 %copy-done.2 = bf16[1,512,2048]{2,1,0:T(8,128)(2,1)S(1)} copy-done((bf16[1,512,2048]{2,1,0:T(8,128)(2,1)S(1)}, bf16[1,512,2048]{2,1,0:T(8,128)(2,1)}, u32[]{:S(2)}) %copy-start.2) | copy-done | bytes 2097176
  64.6 10.1 %expert_work.1 = (bf16[640,2048]{1,0:T(8,128)(2,1)}, bf16[640,2048]{1,0:T(8,128)(2,1)}, bf16[640,512]{1,0:T(8,128)(2,1)}, bf16[640,512]{1,0:T(8,128)(2,1)}, bf16...) custom-call(s32[2]{0:T(128)S(1)} %pad_add_fusion.where_ref, bf16[960,256]{1,0:T(8,128)(2,1)} %copy-done.11, ...), custom_call_target="tpu_custom_call" | custom-call | flops 4026531840 | bytes 12000000 | tf_op jit(solution)/shard_map/expert_work/pallas_call | solution.py:246
  75.7 2.2 %collective-permute-done.16.router_b = f32[8,128]{1,0:T(8,128)S(1)} collective-permute-done((f32[8,128]{1,0:T(8,128)S(1)}, f32[8,128]{1,0:T(8,128)S(1)}, u32[]{:S(2)}, u32[]{:S(2)}) %collective-permute-start.16) | collective-permute-done | bytes 4128 | tf_op jit(solution)/shard_map/ppermute | solution.py:29
  79.3 3.3 %part_work.3 = (bf16[656,256]{1,0:T(8,128)(2,1)S(1)}, bf16[656,256]{1,0:T(8,128)(2,1)S(1)}) custom-call(bf16[640,1024]{1,0:T(8,128)(2,1)} %get-tuple-element.105.grads, bf16[640,1024]{1,0:T(8,128)(2,1)S(1)} %collective-permute-done.15.got, bf16[2,1024,256]{2,1,0:T(8,128)(2,1)S(1)} %copy-done.4, bf16[2,1024,256]{2,1,0:T(8,128)(2,1)} %collective-permute-done.11.given, ...), custom_call_target="tpu_custom_call" | custom-call | flops 1342177280 | bytes 6000000 | tf_op jit(solution)/shard_map/part_work/pallas_call | solution.py:329
  84.0 3.1 %part_work.2 = (bf16[656,256]{1,0:T(8,128)(2,1)S(1)}, f32[640,256]{1,0:T(8,128)S(1)}) custom-call(bf16[640,1024]{1,0:T(8,128)(2,1)} %get-tuple-element.105.grads, bf16[640,1024]{1,0:T(8,128)(2,1)S(1)} %collective-permute-done.15.got, bf16[2,1024,256]{2,1,0:T(8,128)(2,1)S(1)} %copy-done.3, bf16[2,1024,256]{2,1,0:T(8,128)(2,1)} %collective-permute-done.12.given, ...), custom_call_target="tpu_custom_call" | custom-call | flops 1342177280 | bytes 6000000 | tf_op jit(solution)/shard_map/part_work/pallas_call | solution.py:329
  87.2 1.6 %collective-permute-start.19 = (bf16[656,256]{1,0:T(8,128)(2,1)S(1)}, bf16[656,256]{1,0:T(8,128)(2,1)S(1)}, u32[]{:S(2)}, u32[]{:S(2)}) collective-permute-start(bf16[656,256]{1,0:T(8,128)(2,1)S(1)} %get-tuple-element.119), channel_id=1, source_target_pairs={{0,3},{1,0},{2,1},{3,2},{4,7},{5,4},{6,5},{7,6},{8,11},{9,8},{10,9... | collective-permute-start | bytes 1007624 | tf_op jit(solution)/shard_map/ppermute | solution.py:50
  88.8 3.2 %fusion.1 = bf16[1,512,2048]{2,1,0:T(8,128)(2,1)} fusion(bf16[640,512]{1,0:T(8,128)(2,1)S(1)} %copy-done.9, bf16[640,2048]{1,0:T(8,128)(2,1)S(1)} %copy-done.5), kind=kOutput, calls=%fused_computation.4 | convolution fusion | flops 1343225856 | bytes 5373952 | tf_op jit(solution)/shard_map/dot_general | solution.py:67
  92.0 3.2 %fusion = bf16[1,512,2048]{2,1,0:T(8,128)(2,1)} fusion(bf16[640,512]{1,0:T(8,128)(2,1)S(1)} %copy-done.8, bf16[640,2048]{1,0:T(8,128)(2,1)S(1)} %copy-done.5), kind=kOutput, calls=%fused_computation.3 | convolution fusion | flops 1343225856 | bytes 5373952 | tf_op jit(solution)/shard_map/dot_general | solution.py:67
  95.1 6.1 %collective-permute-done.19.refs_2_ = bf16[656,256]{1,0:T(8,128)(2,1)S(1)} collective-permute-done((bf16[656,256]{1,0:T(8,128)(2,1)S(1)}, bf16[656,256]{1,0:T(8,128)(2,1)S(1)}, u32[]{:S(2)}, u32[]{:S(2)}) %collective-permute-start.19) | collective-permute-done | bytes 335904 | tf_op jit(solution)/shard_map/ppermute | solution.py:50
  101.9 2.8 %collective-permute-start.20 = (bf16[176,256]{1,0:T(8,128)(2,1)S(1)}, bf16[176,256]{1,0:T(8,128)(2,1)S(1)}, u32[]{:S(2)}, u32[]{:S(2)}) collective-permute-start(bf16[176,256]{1,0:T(8,128)(2,1)S(1)} %get-tuple-element.125), channel_id=1, source_target_pairs={{0,192},{1,193},{2,194},{3,195},{4,196},{5,197},{6,198},{7,199},{8... | collective-permute-start | bytes 270344 | tf_op jit(solution)/shard_map/ppermute | solution.py:46
  104.8 4.1 %collective-permute-start.21 = (bf16[176,256]{1,0:T(8,128)(2,1)S(1)}, bf16[176,256]{1,0:T(8,128)(2,1)S(1)}, u32[]{:S(2)}, u32[]{:S(2)}) collective-permute-start(bf16[176,256]{1,0:T(8,128)(2,1)S(1)} %get-tuple-element.126), channel_id=1, source_target_pairs={{0,240},{1,241},{2,242},{3,243},{4,244},{5,245},{6,246},{7,247},{8... | collective-permute-start | bytes 270344 | tf_op jit(solution)/shard_map/ppermute | solution.py:46
  108.9 3.2 %fusion.2 = bf16[1,512,2048]{2,1,0:T(8,128)(2,1)} fusion(bf16[640,512]{1,0:T(8,128)(2,1)S(1)} %copy-done.7, bf16[640,2048]{1,0:T(8,128)(2,1)S(1)} %copy-done.6), kind=kOutput, calls=%fused_computation.5 | convolution fusion | flops 1343225856 | bytes 5373952 | tf_op jit(solution)/shard_map/dot_general | solution.py:67
  112.1 6.6 %collective-permute-done.22.refs_2_ = bf16[176,256]{1,0:T(8,128)(2,1)S(1)} collective-permute-done((bf16[176,256]{1,0:T(8,128)(2,1)S(1)}, bf16[176,256]{1,0:T(8,128)(2,1)S(1)}, u32[]{:S(2)}, u32[]{:S(2)}) %collective-permute-start.22) | collective-permute-done | bytes 90144 | tf_op jit(solution)/shard_map/ppermute | solution.py:46
  119.1 1.8 %collective-permute-start.24 = (bf16[256,256]{1,0:T(8,128)(2,1)S(1)}, bf16[256,256]{1,0:T(8,128)(2,1)S(1)}, u32[]{:S(2)}, u32[]{:S(2)}) collective-permute-start(bf16[256,256]{1,0:T(8,128)(2,1)S(1)} %get-tuple-element.138.partial), channel_id=1, source_target_pairs={{0,4},{1,5},{2,6},{3,7},{4,0},{5,1},{6,2},{7,3},{8,12},{9,13},{10,... | collective-permute-start | bytes 393224 | tf_op jit(solution)/shard_map/ppermute | solution.py:54
  122.4 2.2 %collective-permute-done.25 = f32[8,128]{1,0:T(8,128)S(1)} collective-permute-done((f32[8,128]{1,0:T(8,128)S(1)}, f32[8,128]{1,0:T(8,128)S(1)}, u32[]{:S(2)}, u32[]{:S(2)}) %collective-permute-start.25) | collective-permute-done | bytes 4128 | tf_op jit(solution)/shard_map/ppermute | solution.py:58
  126.8 2.7 %collective-permute-start.27 = (bf16[128,256]{1,0:T(8,128)(2,1)S(1)}, bf16[128,256]{1,0:T(8,128)(2,1)S(1)}, u32[]{:S(2)}, u32[]{:S(2)}) collective-permute-start(bf16[128,256]{1,0:T(8,128)(2,1)S(1)} %get-tuple-element.142), channel_id=1, source_target_pairs={{0,8},{8,0},{16,24},{24,16},{32,40},{40,32},{48,56},{56,48},{1,9},... | collective-permute-start | bytes 196616 | tf_op jit(solution)/shard_map/ppermute | solution.py:29
  133.1 2.1 %collective-permute-done.28 = bf16[128,512]{1,0:T(8,128)(2,1)S(1)} collective-permute-done((bf16[128,512]{1,0:T(8,128)(2,1)S(1)}, bf16[128,512]{1,0:T(8,128)(2,1)S(1)}, u32[]{:S(2)}, u32[]{:S(2)}) %collective-permute-start.28) | collective-permute-done | bytes 131104 | tf_op jit(solution)/shard_map/ppermute | solution.py:50
  135.2 2.5 %collective-permute-done.29 = bf16[128,512]{1,0:T(8,128)(2,1)S(1)} collective-permute-done((bf16[128,512]{1,0:T(8,128)(2,1)S(1)}, bf16[128,512]{1,0:T(8,128)(2,1)S(1)}, u32[]{:S(2)}, u32[]{:S(2)}) %collective-permute-start.29) | collective-permute-done | bytes 131104 | tf_op jit(solution)/shard_map/ppermute | solution.py:50
  137.8 3.8 %collective-permute-done.30 = bf16[128,512]{1,0:T(8,128)(2,1)S(1)} collective-permute-done((bf16[128,512]{1,0:T(8,128)(2,1)S(1)}, bf16[128,512]{1,0:T(8,128)(2,1)S(1)}, u32[]{:S(2)}, u32[]{:S(2)}) %collective-permute-start.30) | collective-permute-done | bytes 131104 | tf_op jit(solution)/shard_map/ppermute | solution.py:50
  (103 shorter events, 23.6 us)
Async XLA Ops:
  3.0 1.8 %collective-permute-start = (bf16[144,512]{1,0:T(8,128)(2,1)S(1)}, bf16[144,512]{1,0:T(8,128)(2,1)S(1)}, u32[]{:S(2)}, u32[]{:S(2)}) collective-permute-start(bf16[144,512]{1,0:T(8,128)(2,1)S(1)} %get-tuple-element.157), channel_id=1, source_target_pairs={{0,8},{8,0},{16,24},{24,16},{32,40},{40,32},{48,56},{56,48},{1,9},... | collective-permute-start | bytes 442376 | tf_op jit(solution)/shard_map/ppermute | solution.py:29
  6.0 17.0 %collective-permute-start.1 = (bf16[336,256]{1,0:T(8,128)(2,1)S(1)}, bf16[336,256]{1,0:T(8,128)(2,1)S(1)}, u32[]{:S(2)}, u32[]{:S(2)}) collective-permute-start(bf16[336,256]{1,0:T(8,128)(2,1)S(1)} %get-tuple-element.76), channel_id=1, source_target_pairs={{0,16},{8,24},{16,32},{24,40},{32,48},{40,56},{48,0},{56,8},{1,17}... | collective-permute-start | bytes 516104 | tf_op jit(solution)/shard_map/ppermute | solution.py:34
  9.1 16.9 %collective-permute-start.2 = (bf16[336,256]{1,0:T(8,128)(2,1)S(1)}, bf16[336,256]{1,0:T(8,128)(2,1)S(1)}, u32[]{:S(2)}, u32[]{:S(2)}) collective-permute-start(bf16[336,256]{1,0:T(8,128)(2,1)S(1)} %get-tuple-element.77), channel_id=1, source_target_pairs={{0,36},{1,37},{2,38},{3,39},{4,32},{5,33},{6,34},{7,35},{8,44},{9,... | collective-permute-start | bytes 516104 | tf_op jit(solution)/shard_map/ppermute | solution.py:36
  13.8 15.3 %collective-permute-start.3 = (bf16[336,256]{1,0:T(8,128)(2,1)S(1)}, bf16[336,256]{1,0:T(8,128)(2,1)S(1)}, u32[]{:S(2)}, u32[]{:S(2)}) collective-permute-start(bf16[336,256]{1,0:T(8,128)(2,1)S(1)} %get-tuple-element.78), channel_id=1, source_target_pairs={{0,48},{8,56},{16,0},{24,8},{32,16},{40,24},{48,32},{56,40},{1,49}... | collective-permute-start | bytes 516104 | tf_op jit(solution)/shard_map/ppermute | solution.py:34
  20.3 41.1 %copy-start = (bf16[1,512,2048]{2,1,0:T(8,128)(2,1)S(1)}, bf16[1,512,2048]{2,1,0:T(8,128)(2,1)}, u32[]{:S(2)}) copy-start(bf16[1,512,2048]{2,1,0:T(8,128)(2,1)} %param.11) | copy-start | bytes 6291460
  29.1 11.7 %collective-permute-start.4 = (bf16[960,256]{1,0:T(8,128)(2,1)S(1)}, bf16[960,256]{1,0:T(8,128)(2,1)S(1)}, u32[]{:S(2)}, u32[]{:S(2)}) collective-permute-start(bf16[960,256]{1,0:T(8,128)(2,1)S(1)} %slice_dynamic-update-slice_fusion.refs_0_), channel_id=1, source_target_pairs={{0,1},{1,2},{2,3},{3,0},{4,5},{5,6},{6,7},{7,4},{8,9},{9,10},{10,1... | collective-permute-start | bytes 1474568 | tf_op jit(solution)/shard_map/ppermute | solution.py:50
  29.4 18.2 %collective-permute-start.6 = (bf16[960,256]{1,0:T(8,128)(2,1)S(1)}, bf16[960,256]{1,0:T(8,128)(2,1)}, u32[]{:S(2)}, u32[]{:S(2)}) collective-permute-start(bf16[960,256]{1,0:T(8,128)(2,1)S(1)} %slice_dynamic-update-slice_fusion.refs_0_), channel_id=1, source_target_pairs={{0,3},{1,0},{2,1},{3,2},{4,7},{5,4},{6,5},{7,6},{8,11},{9,8},{10,9... | collective-permute-start | bytes 1474568 | tf_op jit(solution)/shard_map/ppermute | solution.py:50
  30.7 24.2 %collective-permute-start.5 = (bf16[960,256]{1,0:T(8,128)(2,1)S(1)}, bf16[960,256]{1,0:T(8,128)(2,1)}, u32[]{:S(2)}, u32[]{:S(2)}) collective-permute-start(bf16[960,256]{1,0:T(8,128)(2,1)S(1)} %slice_dynamic-update-slice_fusion.refs_0_), channel_id=1, source_target_pairs={{0,2},{1,3},{2,0},{3,1},{4,6},{5,7},{6,4},{7,5},{8,10},{9,11},{10,... | collective-permute-start | bytes 1474568 | tf_op jit(solution)/shard_map/ppermute | solution.py:50
  40.8 14.1 %collective-permute-start.13 = (bf16[1152,128]{1,0:T(8,128)(2,1)S(1)}, bf16[1152,128]{1,0:T(8,128)(2,1)S(1)}, u32[]{:S(2)}, u32[]{:S(2)}) collective-permute-start(bf16[1152,128]{1,0:T(8,128)(2,1)S(1)} %get-tuple-element.91), channel_id=1, source_target_pairs={{0,192},{64,0},{128,64},{192,128},{1,193},{65,1},{129,65},{193,129... | collective-permute-start | bytes 884744 | tf_op jit(solution)/shard_map/ppermute | solution.py:58
  43.6 11.8 %collective-permute-start.7 = (bf16[960,256]{1,0:T(8,128)(2,1)S(1)}, bf16[960,256]{1,0:T(8,128)(2,1)S(1)}, u32[]{:S(2)}, u32[]{:S(2)}) collective-permute-start(bf16[960,256]{1,0:T(8,128)(2,1)S(1)} %slice_dynamic-update-slice_fusion.refs_0_), channel_id=1, source_target_pairs={{0,8},{8,0},{16,24},{24,16},{32,40},{40,32},{48,56},{56,48},{1,9},... | collective-permute-start | bytes 1474568 | tf_op jit(solution)/shard_map/ppermute | solution.py:29
  47.6 8.0 %collective-permute-start.8 = (bf16[960,256]{1,0:T(8,128)(2,1)S(1)}, bf16[960,256]{1,0:T(8,128)(2,1)S(1)}, u32[]{:S(2)}, u32[]{:S(2)}) collective-permute-start(bf16[960,256]{1,0:T(8,128)(2,1)S(1)} %collective-permute-done.4.refs_1_), channel_id=1, source_target_pairs={{0,8},{8,0},{16,24},{24,16},{32,40},{40,32},{48,56},{56,48},{1,9},... | collective-permute-start | bytes 1474568 | tf_op jit(solution)/shard_map/ppermute | solution.py:29
  47.6 13.8 %collective-permute-start.11 = (bf16[2,1024,256]{2,1,0:T(8,128)(2,1)}, bf16[2,1024,256]{2,1,0:T(8,128)(2,1)}, u32[]{:S(2)}, u32[]{:S(2)}) collective-permute-start(bf16[2,1024,256]{2,1,0:T(8,128)(2,1)} %get-tuple-element.89), channel_id=1, source_target_pairs={{0,8},{8,0},{16,24},{24,16},{32,40},{40,32},{48,56},{56,48},{1,9},... | collective-permute-start | bytes 3145736 | tf_op jit(solution)/shard_map/ppermute | solution.py:29
  54.9 6.5 %collective-permute-start.12 = (bf16[2,1024,256]{2,1,0:T(8,128)(2,1)}, bf16[2,1024,256]{2,1,0:T(8,128)(2,1)}, u32[]{:S(2)}, u32[]{:S(2)}) collective-permute-start(bf16[2,1024,256]{2,1,0:T(8,128)(2,1)} %get-tuple-element.90), channel_id=1, source_target_pairs={{0,8},{8,0},{16,24},{24,16},{32,40},{40,32},{48,56},{56,48},{1,9},... | collective-permute-start | bytes 3145736 | tf_op jit(solution)/shard_map/ppermute | solution.py:29
  54.9 6.5 %collective-permute-start.14 = (bf16[2,80,2048]{2,1,0:T(8,128)(2,1)}, bf16[2,80,2048]{2,1,0:T(8,128)(2,1)}, u32[]{:S(2)}, u32[]{:S(2)}) collective-permute-start(bf16[2,80,2048]{2,1,0:T(8,128)(2,1)} %local_slots.1.refs_8_), channel_id=1, source_target_pairs={{0,8},{8,0},{16,24},{24,16},{32,40},{40,32},{48,56},{56,48},{1,9},... | collective-permute-start | bytes 1966088 | tf_op jit(solution)/shard_map/ppermute | solution.py:29
  55.4 5.2 %collective-permute-start.10 = (bf16[960,256]{1,0:T(8,128)(2,1)}, bf16[960,256]{1,0:T(8,128)(2,1)}, u32[]{:S(2)}, u32[]{:S(2)}) collective-permute-start(bf16[960,256]{1,0:T(8,128)(2,1)} %collective-permute-done.6.refs_3_), channel_id=1, source_target_pairs={{0,8},{8,0},{16,24},{24,16},{32,40},{40,32},{48,56},{56,48},{1,9},... | collective-permute-start | bytes 1474568 | tf_op jit(solution)/shard_map/ppermute | solution.py:29
  55.6 5.8 %collective-permute-start.9 = (bf16[960,256]{1,0:T(8,128)(2,1)}, bf16[960,256]{1,0:T(8,128)(2,1)}, u32[]{:S(2)}, u32[]{:S(2)}) collective-permute-start(bf16[960,256]{1,0:T(8,128)(2,1)} %collective-permute-done.5.refs_2_), channel_id=1, source_target_pairs={{0,8},{8,0},{16,24},{24,16},{32,40},{40,32},{48,56},{56,48},{1,9},... | collective-permute-start | bytes 1474568 | tf_op jit(solution)/shard_map/ppermute | solution.py:29
  74.7 3.3 %collective-permute-start.15 = (bf16[640,1024]{1,0:T(8,128)(2,1)}, bf16[640,1024]{1,0:T(8,128)(2,1)S(1)}, u32[]{:S(2)}, u32[]{:S(2)}) collective-permute-start(bf16[640,1024]{1,0:T(8,128)(2,1)} %get-tuple-element.105.grads), channel_id=1, source_target_pairs={{0,8},{8,0},{16,24},{24,16},{32,40},{40,32},{48,56},{56,48},{1,9},... | collective-permute-start | bytes 3932168 | tf_op jit(solution)/shard_map/ppermute | solution.py:29
  75.4 2.4 %collective-permute-start.16 = (f32[8,128]{1,0:T(8,128)S(1)}, f32[8,128]{1,0:T(8,128)S(1)}, u32[]{:S(2)}, u32[]{:S(2)}) collective-permute-start(f32[8,128]{1,0:T(8,128)S(1)} %pad.9.router_a), channel_id=1, source_target_pairs={{0,8},{8,0},{16,24},{24,16},{32,40},{40,32},{48,56},{56,48},{1,9},... | collective-permute-start | bytes 12296 | tf_op jit(solution)/shard_map/ppermute | solution.py:29
  82.6 12.6 %collective-permute-start.17 = (bf16[656,256]{1,0:T(8,128)(2,1)S(1)}, bf16[656,256]{1,0:T(8,128)(2,1)S(1)}, u32[]{:S(2)}, u32[]{:S(2)}) collective-permute-start(bf16[656,256]{1,0:T(8,128)(2,1)S(1)} %get-tuple-element.117), channel_id=1, source_target_pairs={{0,1},{1,2},{2,3},{3,0},{4,5},{5,6},{6,7},{7,4},{8,9},{9,10},{10,1... | collective-permute-start | bytes 1007624 | tf_op jit(solution)/shard_map/ppermute | solution.py:50
  82.7 12.5 %collective-permute-start.18 = (bf16[656,256]{1,0:T(8,128)(2,1)S(1)}, bf16[656,256]{1,0:T(8,128)(2,1)S(1)}, u32[]{:S(2)}, u32[]{:S(2)}) collective-permute-start(bf16[656,256]{1,0:T(8,128)(2,1)S(1)} %get-tuple-element.118), channel_id=1, source_target_pairs={{0,2},{1,3},{2,0},{3,1},{4,6},{5,7},{6,4},{7,5},{8,10},{9,11},{10,... | collective-permute-start | bytes 1007624 | tf_op jit(solution)/shard_map/ppermute | solution.py:50
  87.2 14.1 %collective-permute-start.19 = (bf16[656,256]{1,0:T(8,128)(2,1)S(1)}, bf16[656,256]{1,0:T(8,128)(2,1)S(1)}, u32[]{:S(2)}, u32[]{:S(2)}) collective-permute-start(bf16[656,256]{1,0:T(8,128)(2,1)S(1)} %get-tuple-element.119), channel_id=1, source_target_pairs={{0,3},{1,0},{2,1},{3,2},{4,7},{5,4},{6,5},{7,6},{8,11},{9,8},{10,9... | collective-permute-start | bytes 1007624 | tf_op jit(solution)/shard_map/ppermute | solution.py:50
  101.9 10.1 %collective-permute-start.20 = (bf16[176,256]{1,0:T(8,128)(2,1)S(1)}, bf16[176,256]{1,0:T(8,128)(2,1)S(1)}, u32[]{:S(2)}, u32[]{:S(2)}) collective-permute-start(bf16[176,256]{1,0:T(8,128)(2,1)S(1)} %get-tuple-element.125), channel_id=1, source_target_pairs={{0,192},{1,193},{2,194},{3,195},{4,196},{5,197},{6,198},{7,199},{8... | collective-permute-start | bytes 270344 | tf_op jit(solution)/shard_map/ppermute | solution.py:46
  104.8 7.3 %collective-permute-start.21 = (bf16[176,256]{1,0:T(8,128)(2,1)S(1)}, bf16[176,256]{1,0:T(8,128)(2,1)S(1)}, u32[]{:S(2)}, u32[]{:S(2)}) collective-permute-start(bf16[176,256]{1,0:T(8,128)(2,1)S(1)} %get-tuple-element.126), channel_id=1, source_target_pairs={{0,240},{1,241},{2,242},{3,243},{4,244},{5,245},{6,246},{7,247},{8... | collective-permute-start | bytes 270344 | tf_op jit(solution)/shard_map/ppermute | solution.py:46
  108.9 9.8 %collective-permute-start.22 = (bf16[176,256]{1,0:T(8,128)(2,1)S(1)}, bf16[176,256]{1,0:T(8,128)(2,1)S(1)}, u32[]{:S(2)}, u32[]{:S(2)}) collective-permute-start(bf16[176,256]{1,0:T(8,128)(2,1)S(1)} %get-tuple-element.127), channel_id=1, source_target_pairs={{0,228},{1,229},{2,230},{3,231},{4,224},{5,225},{6,226},{7,227},{8... | collective-permute-start | bytes 270344 | tf_op jit(solution)/shard_map/ppermute | solution.py:46
  108.9 9.8 %collective-permute-start.23 = (bf16[176,256]{1,0:T(8,128)(2,1)S(1)}, bf16[176,256]{1,0:T(8,128)(2,1)S(1)}, u32[]{:S(2)}, u32[]{:S(2)}) collective-permute-start(bf16[176,256]{1,0:T(8,128)(2,1)S(1)} %get-tuple-element.128), channel_id=1, source_target_pairs={{0,208},{1,209},{2,210},{3,211},{4,212},{5,213},{6,214},{7,215},{8... | collective-permute-start | bytes 270344 | tf_op jit(solution)/shard_map/ppermute | solution.py:46
  119.1 7.1 %collective-permute-start.24 = (bf16[256,256]{1,0:T(8,128)(2,1)S(1)}, bf16[256,256]{1,0:T(8,128)(2,1)S(1)}, u32[]{:S(2)}, u32[]{:S(2)}) collective-permute-start(bf16[256,256]{1,0:T(8,128)(2,1)S(1)} %get-tuple-element.138.partial), channel_id=1, source_target_pairs={{0,4},{1,5},{2,6},{3,7},{4,0},{5,1},{6,2},{7,3},{8,12},{9,13},{10,... | collective-permute-start | bytes 393224 | tf_op jit(solution)/shard_map/ppermute | solution.py:54
  120.9 3.7 %collective-permute-start.25 = (f32[8,128]{1,0:T(8,128)S(1)}, f32[8,128]{1,0:T(8,128)S(1)}, u32[]{:S(2)}, u32[]{:S(2)}) collective-permute-start(f32[8,128]{1,0:T(8,128)S(1)} %get-tuple-element.141), channel_id=1, source_target_pairs={{0,64},{64,128},{128,192},{192,0},{1,65},{65,129},{129,193},{193,1... | collective-permute-start | bytes 12296 | tf_op jit(solution)/shard_map/ppermute | solution.py:58
  121.6 4.6 %collective-permute-start.26 = (f32[8,128]{1,0:T(8,128)S(1)}, f32[8,128]{1,0:T(8,128)S(1)}, u32[]{:S(2)}, u32[]{:S(2)}) collective-permute-start(f32[8,128]{1,0:T(8,128)S(1)} %get-tuple-element.141), channel_id=1, source_target_pairs={{0,68},{1,69},{2,70},{3,71},{4,64},{5,65},{6,66},{7,67},{64,132},{... | collective-permute-start | bytes 12296 | tf_op jit(solution)/shard_map/ppermute | solution.py:63
  126.8 3.6 %collective-permute-start.27 = (bf16[128,256]{1,0:T(8,128)(2,1)S(1)}, bf16[128,256]{1,0:T(8,128)(2,1)S(1)}, u32[]{:S(2)}, u32[]{:S(2)}) collective-permute-start(bf16[128,256]{1,0:T(8,128)(2,1)S(1)} %get-tuple-element.142), channel_id=1, source_target_pairs={{0,8},{8,0},{16,24},{24,16},{32,40},{40,32},{48,56},{56,48},{1,9},... | collective-permute-start | bytes 196616 | tf_op jit(solution)/shard_map/ppermute | solution.py:29
  130.4 4.8 %collective-permute-start.28 = (bf16[128,512]{1,0:T(8,128)(2,1)S(1)}, bf16[128,512]{1,0:T(8,128)(2,1)S(1)}, u32[]{:S(2)}, u32[]{:S(2)}) collective-permute-start(bf16[128,512]{1,0:T(8,128)(2,1)S(1)} %get-tuple-element.153), channel_id=1, source_target_pairs={{0,1},{1,2},{2,3},{3,0},{4,5},{5,6},{6,7},{7,4},{8,9},{9,10},{10,1... | collective-permute-start | bytes 393224 | tf_op jit(solution)/shard_map/ppermute | solution.py:50
  131.9 5.9 %collective-permute-start.29 = (bf16[128,512]{1,0:T(8,128)(2,1)S(1)}, bf16[128,512]{1,0:T(8,128)(2,1)S(1)}, u32[]{:S(2)}, u32[]{:S(2)}) collective-permute-start(bf16[128,512]{1,0:T(8,128)(2,1)S(1)} %get-tuple-element.153), channel_id=1, source_target_pairs={{0,2},{1,3},{2,0},{3,1},{4,6},{5,7},{6,4},{7,5},{8,10},{9,11},{10,... | collective-permute-start | bytes 393224 | tf_op jit(solution)/shard_map/ppermute | solution.py:50
  132.4 9.1 %collective-permute-start.30 = (bf16[128,512]{1,0:T(8,128)(2,1)S(1)}, bf16[128,512]{1,0:T(8,128)(2,1)S(1)}, u32[]{:S(2)}, u32[]{:S(2)}) collective-permute-start(bf16[128,512]{1,0:T(8,128)(2,1)S(1)} %get-tuple-element.153), channel_id=1, source_target_pairs={{0,3},{1,0},{2,1},{3,2},{4,7},{5,4},{6,5},{7,6},{8,11},{9,8},{10,9... | collective-permute-start | bytes 393224 | tf_op jit(solution)/shard_map/ppermute | solution.py:50
  (14 other events, 111.6 us)
where the time goes:
time: 143 us; the launch traced here: 142 us
  waiting for transfers between devices  48.9 us (34%)
  starting transfers between devices  46.2 us (32%)
  Pallas kernels  26.3 us (18%)
  matrix products  9.51 us (7%)
  local copies, waits for them, and re-layouts  8.3 us (6%)
  other arithmetic  2.27 us (2%)
    ppermute x9, waiting for transfers between devices, x_shift(): lax.ppermute(a, 'dp', [(i, i // 4 * 4 + (i + j) % 4) for i in range(8)])  23.6 us
    ppermute x11, starting transfers between devices, core_swap(): return lax.ppermute(a, 'expert', [(i, i ^ 1) for i in range(8)])  16.4 us
    pallas_call x1, Pallas kernels, expert_work(): pl.pallas_call(expert_kernel, out_shape=[pltpu.HBM((ROWS, D), BF), pltpu....  10.1 us
    dot_general x3, matrix products, dot(): return lax.dot_general(a, b, (dims, ((), ())), preferred_element_type=F32)  9.51 us
    ppermute x11, waiting for transfers between devices, core_swap(): return lax.ppermute(a, 'expert', [(i, i ^ 1) for i in range(8)])  8.96 us
    unnamed x35, local copies, waits for them, and re-layouts  7 us
    ppermute x4, starting transfers between devices, chip_return(): return lax.ppermute(a, ('section', 'expert', 'dp'), route)  6.96 us
    ppermute x4, waiting for transfers between devices, chip_return(): return lax.ppermute(a, ('section', 'expert', 'dp'), route)  6.63 us
  transfers between devices with their start and end apart: 31, of which 16 were waited for; matrix products, arithmetic and copies ran while one was open for 7% of the time, Pallas kernels for 7%

commit v1 on v0

--- a/solution.py
+++ b/solution.py
@@ -56,11 +56,6 @@
 
 def section_shift(a, by):
     return lax.ppermute(a, "section", [(s, (s + by) % 4) for s in range(4)])
-
-
-def next_section_pair(a):
-    route = [(s * 8 + d, (s + 1) % 4 * 8 + (d + 4) % 8) for s in range(4) for d in range(8)]
-    return lax.ppermute(a, ("section", "dp"), route)
 
 
 def dot(a, b, dims):
@@ -342,7 +337,7 @@
     return jnp.concatenate([high.astype(F32), value - high.astype(F32)]).astype(BF)
 
 
-def x_sum_kernel(where_ref, keep, router_a, router_b, *refs):
+def x_sum_kernel(blocks, where_ref, keep, router_a, router_b, *refs):
     arrived, outs = refs[:3], refs[3:]
     x = where_ref[0]
     own = hi_lo(router_a[...] + router_b[...]).astype(F32)
@@ -356,22 +351,22 @@
             picked = jnp.where(j == k, tails[k], picked)
         total = total + picked
     tail = hi_lo(total)
-    for r in range(EXPERTS):
+    for r, out in zip(blocks, outs):
         rows = slice(r * PAIR, r * PAIR + PAIR)
         block = keep[rows, :]
         for a in arrived:
             block = block + a[rows, :].astype(F32)
-        outs[r][:PAIR, :] = block.astype(BF)
-        outs[r][PAIR:, :TOK] = tail
-        outs[r][PAIR:, TOK:] = jnp.zeros((16, TOK), BF)
-
-
-def x_sum(where, keep, router_a, router_b, arrived):
-    return pl.pallas_call(
-        x_sum_kernel,
-        out_shape=[jax.ShapeDtypeStruct((PAIR + 16, 256), BF)] * 4,
+        out[:PAIR, :] = block.astype(BF)
+        out[PAIR:, :TOK] = tail
+        out[PAIR:, TOK:] = jnp.zeros((16, TOK), BF)
+
+
+def x_sum(blocks, where, keep, router_a, router_b, arrived):
+    return pl.pallas_call(
+        functools.partial(x_sum_kernel, blocks),
+        out_shape=[jax.ShapeDtypeStruct((PAIR + 16, 256), BF)] * len(blocks),
         in_specs=[SMEM] + [VMEM] * 6,
-        out_specs=[BLOCK] * 4,
+        out_specs=[BLOCK] * len(blocks),
         compiler_params=params(8),
         cost_estimate=cost(1_000_000, 3_000_000),
         name="x_sum",
@@ -379,7 +374,7 @@
 
 
 def return_kernel(*refs):
-    parts, (pack, out_ref, router_ref) = refs[:4], refs[4:]
+    parts, (pack, out_ref) = refs[:4], refs[4:]
     row = lax.broadcasted_iota(jnp.int32, (8, TOK), 0)
     router = jnp.zeros((8, TOK), F32)
     for c in range(2):
@@ -393,25 +388,23 @@
             value = tail[at : at + 1] + tail[8 + at : 9 + at]
             router = jnp.where(row == 4 * c + r, value, router)
         out_ref[c * TOK : (c + 1) * TOK, :] = total.astype(BF)
-    router_ref[...] = router
+    out_ref[2 * TOK :, :TOK] = hi_lo(router)
+    out_ref[2 * TOK :, TOK:] = jnp.zeros((16, TOK), BF)
 
 
 def return_slots(parts, pack):
     return pl.pallas_call(
         return_kernel,
-        out_shape=[
-            jax.ShapeDtypeStruct((2 * TOK, 256), BF),
-            jax.ShapeDtypeStruct((8, TOK), F32),
-        ],
+        out_shape=jax.ShapeDtypeStruct((2 * TOK + 16, 256), BF),
         in_specs=[BLOCK] * 5,
-        out_specs=[BLOCK] * 2,
+        out_specs=BLOCK,
         compiler_params=params(8),
         cost_estimate=cost(100_000_000, 1_500_000),
         name="return_slots",
     )(*parts, pack)
 
 
-def final_kernel(where_ref, partial, got, pack, stays, goes):
+def final_kernel(where_ref, partial, got, pack, stays, goes, router):
     core = where_ref[1]
     total = partial[...].astype(F32) + got[...].astype(F32)
     final = []
@@ -425,6 +418,8 @@
         columns = slice(h * TOK, h * TOK + TOK)
         stays[:, columns] = jnp.where(core == 0, final[h], final[2 + h]).astype(BF)
         goes[:, columns] = jnp.where(core == 0, final[2 + h], final[h]).astype(BF)
+    tail = total[2 * TOK :, :TOK]
+    router[...] = tail[:8] + tail[8:]
 
 
 def finish(where, partial, got, pack):
@@ -433,9 +428,10 @@
         out_shape=[
             jax.ShapeDtypeStruct((TOK, 256), BF),
             jax.ShapeDtypeStruct((TOK, 256), BF),
+            jax.ShapeDtypeStruct((8, TOK), F32),
         ],
         in_specs=[SMEM] + [BLOCK] * 3,
-        out_specs=[BLOCK] * 2,
+        out_specs=[BLOCK] * 3,
         compiler_params=params(8),
         cost_estimate=cost(1_000_000, 600_000),
         name="finish",
@@ -485,14 +481,16 @@
     local = [local, core_swap(local)]
     rows = [z[:PAIR] for z in away] + [z[PAIR : 2 * PAIR] for z in away]
     pieces = x_gather(jnp.concatenate(rows))
+    given = [core_swap(g) for g in given]
     own, near, given, pack = lax.optimization_barrier((pieces[0], pieces[1], given, pack))
     pack = section_shift(pack, -1)
-    given = [pinned(core_swap(g)) for g in given]
+    given = [pinned(g) for g in given]
+    pieces[2], pieces[3], pack = lax.optimization_barrier((pieces[2], pieces[3], pack))
     pieces[:2] = own, near
     gates = jnp.stack([gate0[:2, :CAP]] + [z[2 * PAIR : 2 * PAIR + 2, :CAP] for z in away])
     gates = gates.astype(F32).reshape(ROWS, 1)
     pieces = pieces + [core_swap(p) for p in pieces]
-    pieces, given, pack = lax.optimization_barrier((pieces, given, pack))
+    pieces, given = lax.optimization_barrier((pieces, given))
 
     rows_input, rows_grad, gpg, upg, scaled, router, half = expert_work(
         where, pieces, local, w_gate[0], w_up[0], w_down[0], gates
@@ -507,16 +505,18 @@
     arrived = [near, far, x_shift(back, 3)]
     grads = [weight_grad(gpg, rows_input), weight_grad(upg, rows_input)]
     keep, grads = lax.optimization_barrier((keep, grads))
-    blocks = x_sum(where, keep, *routers, arrived)
+    (far_block,) = x_sum((2,), where, keep, *routers, arrived)
+    far_block, keep = lax.optimization_barrier((far_block, keep))
+    blocks = x_sum((0, 1, 3), where, keep, *routers, arrived)
     blocks, scaled = lax.optimization_barrier((blocks, scaled))
+    blocks = {0: blocks[0], 1: blocks[1], 3: blocks[2], 2: far_block}
     blocks = [chip_return(blocks[r], r) for r in range(EXPERTS)]
     grads.append(weight_grad(scaled, rows_grad))
     blocks, grads = lax.optimization_barrier((blocks, grads))
 
-    partial, by_expert = return_slots(blocks, pack)
-    by_expert = section_shift(by_expert, 1) + next_section_pair(by_expert)
-    stays, goes = finish(where, partial, pair_swap(partial), pack)
-    goes, by_expert = lax.optimization_barrier((goes, by_expert))
+    partial = return_slots(blocks, pack)
+    stays, goes, by_expert = finish(where, partial, pair_swap(partial), pack)
+    by_expert = section_shift(by_expert, 1)
     goes = core_swap(goes)
     low = jnp.where(core == 0, stays, goes)
     high = jnp.where(core == 0, goes, stays)

time: 143 us -> 140 us (0.979)
  starting transfers between devices: 46.2 us -> 37.7 us
  waiting for transfers between devices: 48.9 us -> 53.3 us
    ppermute x9, waiting for transfers between devices: 23.6 us -> 30.4 us  [x_shift(): lax.ppermute(a, 'dp', [(i, i // 4 * 4 + (i + j) % 4) for i in range(8)])]
    ppermute x11, starting transfers between devices: 16.4 us -> 10.2 us  [core_swap(): return lax.ppermute(a, 'expert', [(i, i ^ 1) for i in range(8)])]
    ppermute x1, waiting for transfers between devices: 0.01 us -> 2.82 us  [pair_swap(): return lax.ppermute(a, 'dp', [(i, (i + 4) % 8) for i in range(8)])]
    ppermute x11, waiting for transfers between devices: 8.96 us -> 6.41 us  [core_swap(): return lax.ppermute(a, 'expert', [(i, i ^ 1) for i in range(8)])]
    ppermute x4, waiting for transfers between devices: 6.63 us -> 5.09 us  [chip_return(): return lax.ppermute(a, ('section', 'expert', 'dp'), route)]
    ppermute x1 -> x0, waiting for transfers between devices: 1.55 us -> none  [next_section_pair(): return lax.ppermute(a, ('section', 'dp'), route)]
    unnamed x35 -> x33, local copies, waits for them, and re-layouts: 7 us -> 6.49 us
  transfers between devices with their start and end apart: 31 -> 30, of which waited for: 16 -> 18; matrix products, arithmetic and copies ran while one was open for 7% -> 8% of each run, Pallas kernels for 7% -> 7%
where the time goes in v1:
time: 140 us; the launch traced here: 138 us
  waiting for transfers between devices  53.3 us (38%)
  starting transfers between devices  37.7 us (27%)
  Pallas kernels  26.8 us (19%)
  matrix products  9.44 us (7%)
  local copies, waits for them, and re-layouts  7.79 us (6%)
  other arithmetic  2.26 us (2%)
    ppermute x9, waiting for transfers between devices, x_shift(): lax.ppermute(a, 'dp', [(i, i // 4 * 4 + (i + j) % 4) for i in range(8)])  30.4 us
    ppermute x11, starting transfers between devices, core_swap(): return lax.ppermute(a, 'expert', [(i, i ^ 1) for i in range(8)])  10.2 us
    pallas_call x1, Pallas kernels, expert_work(): pl.pallas_call(expert_kernel, out_shape=[pltpu.HBM((ROWS, D), BF), pltpu....  10.1 us
    dot_general x3, matrix products, dot(): return lax.dot_general(a, b, (dims, ((), ())), preferred_element_type=F32)  9.44 us
    ppermute x9, starting transfers between devices, x_shift(): lax.ppermute(a, 'dp', [(i, i // 4 * 4 + (i + j) % 4) for i in range(8)])  6.68 us
    ppermute x4, starting transfers between devices, chip_return(): return lax.ppermute(a, ('section', 'expert', 'dp'), route)  6.59 us
    unnamed x33, local copies, waits for them, and re-layouts  6.49 us
    pallas_call x2, Pallas kernels, part_work(): pl.pallas_call(functools.partial(part_kernel, chunks), out_shape=shapes,...  6.42 us
  transfers between devices with their start and end apart: 30, of which 18 were waited for; matrix products, arithmetic and copies ran while one was open for 8% of the time, Pallas kernels for 7%

profile of v1, /device:TPU:7, one launch (start us, length us, event | category | flops | bytes accessed | tf_op | source)
XLA Modules:
  0.0 138.3 jit_solution(10481872716565656276)
XLA Ops:
  6.0 3.1 %collective-permute-start.1 = (bf16[336,256]{1,0:T(8,128)(2,1)S(1)}, bf16[336,256]{1,0:T(8,128)(2,1)S(1)}, u32[]{:S(2)}, u32[]{:S(2)}) collective-permute-start(bf16[336,256]{1,0:T(8,128)(2,1)S(1)} %get-tuple-element.75), channel_id=1, source_target_pairs={{0,16},{8,24},{16,32},{24,40},{32,48},{40,56},{48,0},{56,8},{1,17}... | collective-permute-start | bytes 516104 | tf_op jit(solution)/shard_map/ppermute | solution.py:34
  9.1 4.7 %collective-permute-start.2 = (bf16[336,256]{1,0:T(8,128)(2,1)S(1)}, bf16[336,256]{1,0:T(8,128)(2,1)S(1)}, u32[]{:S(2)}, u32[]{:S(2)}) collective-permute-start(bf16[336,256]{1,0:T(8,128)(2,1)S(1)} %get-tuple-element.76), channel_id=1, source_target_pairs={{0,36},{1,37},{2,38},{3,39},{4,32},{5,33},{6,34},{7,35},{8,44},{9,... | collective-permute-start | bytes 516104 | tf_op jit(solution)/shard_map/ppermute | solution.py:36
  13.8 2.4 %collective-permute-start.3 = (bf16[336,256]{1,0:T(8,128)(2,1)S(1)}, bf16[336,256]{1,0:T(8,128)(2,1)S(1)}, u32[]{:S(2)}, u32[]{:S(2)}) collective-permute-start(bf16[336,256]{1,0:T(8,128)(2,1)S(1)} %get-tuple-element.77), channel_id=1, source_target_pairs={{0,48},{8,56},{16,0},{24,8},{32,16},{40,24},{48,32},{56,40},{1,49}... | collective-permute-start | bytes 516104 | tf_op jit(solution)/shard_map/ppermute | solution.py:34
  16.1 4.2 %arrange_weights.1 = (bf16[2,1024,256]{2,1,0:T(8,128)(2,1)}, bf16[2,1024,256]{2,1,0:T(8,128)(2,1)}, bf16[2,1024,256]{2,1,0:T(8,128)(2,1)}, bf16[2,1024,256]{2,1,0:T(8,128)(2,1)}) custom-call(s32[2]{0:T(128)S(1)} %pad_add_fusion.where_ref, bf16[512,2048]{1,0:T(8,128)(2,1)} %bitcast.30, bf16[512,2048]{1,0:T(8,128)(2,1)} %bitcast.32), custom_call_target="tpu_custom_call" | custom-call | bytes 8000000 | tf_op jit(solution)/shard_map/arrange_weights/pallas_call | solution.py:289
  20.3 2.7 %local_slots.1.refs_8_ = bf16[2,80,2048]{2,1,0:T(8,128)(2,1)} custom-call(bf16[144,512]{1,0:T(8,128)(2,1)S(1)} %get-tuple-element.156.mine_ref, bf16[128,2048]{1,0:T(8,128)(2,1)} %input_ref.1, bf16[128,2048]{1,0:T(8,128)(2,1)} %grad_ref.1), custom_call_target="tpu_custom_call" | custom-call | flops 100000000 | bytes 2000000 | tf_op jit(solution)/shard_map/local_slots/pallas_call | solution.py:150
  23.0 3.0 %collective-permute-done.2 = bf16[336,256]{1,0:T(8,128)(2,1)S(1)} collective-permute-done((bf16[336,256]{1,0:T(8,128)(2,1)S(1)}, bf16[336,256]{1,0:T(8,128)(2,1)S(1)}, u32[]{:S(2)}, u32[]{:S(2)}) %collective-permute-start.2) | collective-permute-done | bytes 172064 | tf_op jit(solution)/shard_map/ppermute | solution.py:36
  26.0 3.0 %collective-permute-done.3 = bf16[336,256]{1,0:T(8,128)(2,1)S(1)} collective-permute-done((bf16[336,256]{1,0:T(8,128)(2,1)S(1)}, bf16[336,256]{1,0:T(8,128)(2,1)S(1)}, u32[]{:S(2)}, u32[]{:S(2)}) %collective-permute-start.3) | collective-permute-done | bytes 172064 | tf_op jit(solution)/shard_map/ppermute | solution.py:34
  30.7 2.1 %collective-permute-start.7 = (bf16[960,256]{1,0:T(8,128)(2,1)S(1)}, bf16[960,256]{1,0:T(8,128)(2,1)}, u32[]{:S(2)}, u32[]{:S(2)}) collective-permute-start(bf16[960,256]{1,0:T(8,128)(2,1)S(1)} %slice_dynamic-update-slice_fusion.refs_0_), channel_id=1, source_target_pairs={{0,2},{1,3},{2,0},{3,1},{4,6},{5,7},{6,4},{7,5},{8,10},{9,11},{10,... | collective-permute-start | bytes 1474568 | tf_op jit(solution)/shard_map/ppermute | solution.py:50
  32.8 10.1 %collective-permute-done.4.refs_1_ = bf16[960,256]{1,0:T(8,128)(2,1)} collective-permute-done((bf16[960,256]{1,0:T(8,128)(2,1)S(1)}, bf16[960,256]{1,0:T(8,128)(2,1)}, u32[]{:S(2)}, u32[]{:S(2)}) %collective-permute-start.4) | collective-permute-done | bytes 491552 | tf_op jit(solution)/shard_map/ppermute | solution.py:50
  43.0 2.8 %collective-permute-start.9 = (bf16[1152,128]{1,0:T(8,128)(2,1)S(1)}, bf16[1152,128]{1,0:T(8,128)(2,1)S(1)}, u32[]{:S(2)}, u32[]{:S(2)}) collective-permute-start(bf16[1152,128]{1,0:T(8,128)(2,1)S(1)} %get-tuple-element.88), channel_id=1, source_target_pairs={{0,192},{64,0},{128,64},{192,128},{1,193},{65,1},{129,65},{193,129... | collective-permute-start | bytes 884744 | tf_op jit(solution)/shard_map/ppermute | solution.py:58
  45.8 2.4 %collective-permute-start.14 = (bf16[2,80,2048]{2,1,0:T(8,128)(2,1)}, bf16[2,80,2048]{2,1,0:T(8,128)(2,1)}, u32[]{:S(2)}, u32[]{:S(2)}) collective-permute-start(bf16[2,80,2048]{2,1,0:T(8,128)(2,1)} %local_slots.1.refs_8_), channel_id=1, source_target_pairs={{0,8},{8,0},{16,24},{24,16},{32,40},{40,32},{48,56},{56,48},{1,9},... | collective-permute-start | bytes 1966088 | tf_op jit(solution)/shard_map/ppermute | solution.py:29
  48.7 7.3 %collective-permute-done.8.refs_3_ = bf16[960,256]{1,0:T(8,128)(2,1)} collective-permute-done((bf16[960,256]{1,0:T(8,128)(2,1)S(1)}, bf16[960,256]{1,0:T(8,128)(2,1)}, u32[]{:S(2)}, u32[]{:S(2)}) %collective-permute-start.8) | collective-permute-done | bytes 491552 | tf_op jit(solution)/shard_map/ppermute | solution.py:50
  56.7 1.6 %collective-permute-done.12.refs_6_ = bf16[960,256]{1,0:T(8,128)(2,1)} collective-permute-done((bf16[960,256]{1,0:T(8,128)(2,1)}, bf16[960,256]{1,0:T(8,128)(2,1)}, u32[]{:S(2)}, u32[]{:S(2)}) %collective-permute-start.12) | collective-permute-done | bytes 491552 | tf_op jit(solution)/shard_map/ppermute | solution.py:29
  59.0 1.6 %copy-done.1 = bf16[1,512,2048]{2,1,0:T(8,128)(2,1)S(1)} copy-done((bf16[1,512,2048]{2,1,0:T(8,128)(2,1)S(1)}, bf16[1,512,2048]{2,1,0:T(8,128)(2,1)}, u32[]{:S(2)}) %copy-start.1) | copy-done | bytes 2097176
  60.6 1.6 %copy-done.2 = bf16[1,512,2048]{2,1,0:T(8,128)(2,1)S(1)} copy-done((bf16[1,512,2048]{2,1,0:T(8,128)(2,1)S(1)}, bf16[1,512,2048]{2,1,0:T(8,128)(2,1)}, u32[]{:S(2)}) %copy-start.2) | copy-done | bytes 2097176
  62.2 10.1 %expert_work.1 = (bf16[640,2048]{1,0:T(8,128)(2,1)}, bf16[640,2048]{1,0:T(8,128)(2,1)}, bf16[640,512]{1,0:T(8,128)(2,1)}, bf16[640,512]{1,0:T(8,128)(2,1)}, bf16...) custom-call(s32[2]{0:T(128)S(1)} %pad_add_fusion.where_ref, bf16[960,256]{1,0:T(8,128)(2,1)} %copy-done.11, ...), custom_call_target="tpu_custom_call" | custom-call | flops 4026531840 | bytes 12000000 | tf_op jit(solution)/shard_map/expert_work/pallas_call | solution.py:241
  73.3 2.2 %collective-permute-done.16.router_b = f32[8,128]{1,0:T(8,128)S(1)} collective-permute-done((f32[8,128]{1,0:T(8,128)S(1)}, f32[8,128]{1,0:T(8,128)S(1)}, u32[]{:S(2)}, u32[]{:S(2)}) %collective-permute-start.16) | collective-permute-done | bytes 4128 | tf_op jit(solution)/shard_map/ppermute | solution.py:29
  76.9 3.3 %part_work.3 = (bf16[656,256]{1,0:T(8,128)(2,1)S(1)}, bf16[656,256]{1,0:T(8,128)(2,1)S(1)}) custom-call(bf16[640,1024]{1,0:T(8,128)(2,1)} %get-tuple-element.106.grads, bf16[640,1024]{1,0:T(8,128)(2,1)S(1)} %collective-permute-done.15.got, bf16[2,1024,256]{2,1,0:T(8,128)(2,1)S(1)} %copy-done.4, bf16[2,1024,256]{2,1,0:T(8,128)(2,1)} %copy-done.13, ...), custom_call_target="tpu_custom_call" | custom-call | flops 1342177280 | bytes 6000000 | tf_op jit(solution)/shard_map/part_work/pallas_call | solution.py:324
  84.0 3.1 %part_work.2 = (bf16[656,256]{1,0:T(8,128)(2,1)S(1)}, f32[640,256]{1,0:T(8,128)S(1)}) custom-call(bf16[640,1024]{1,0:T(8,128)(2,1)} %get-tuple-element.106.grads, bf16[640,1024]{1,0:T(8,128)(2,1)S(1)} %collective-permute-done.15.got, bf16[2,1024,256]{2,1,0:T(8,128)(2,1)S(1)} %copy-done.3, bf16[2,1024,256]{2,1,0:T(8,128)(2,1)} %copy-done.12, ...), custom_call_target="tpu_custom_call" | custom-call | flops 1342177280 | bytes 6000000 | tf_op jit(solution)/shard_map/part_work/pallas_call | solution.py:324
  87.4 3.2 %fusion.1 = bf16[1,512,2048]{2,1,0:T(8,128)(2,1)} fusion(bf16[640,512]{1,0:T(8,128)(2,1)S(1)} %copy-done.9, bf16[640,2048]{1,0:T(8,128)(2,1)S(1)} %copy-done.5), kind=kOutput, calls=%fused_computation.4 | convolution fusion | flops 1343225856 | bytes 5373952 | tf_op jit(solution)/shard_map/dot_general | solution.py:62
  90.6 3.1 %fusion = bf16[1,512,2048]{2,1,0:T(8,128)(2,1)} fusion(bf16[640,512]{1,0:T(8,128)(2,1)S(1)} %copy-done.8, bf16[640,2048]{1,0:T(8,128)(2,1)S(1)} %copy-done.5), kind=kOutput, calls=%fused_computation.3 | convolution fusion | flops 1343225856 | bytes 5373952 | tf_op jit(solution)/shard_map/dot_general | solution.py:62
  93.7 6.1 %collective-permute-done.19.refs_2_ = bf16[656,256]{1,0:T(8,128)(2,1)S(1)} collective-permute-done((bf16[656,256]{1,0:T(8,128)(2,1)S(1)}, bf16[656,256]{1,0:T(8,128)(2,1)S(1)}, u32[]{:S(2)}, u32[]{:S(2)}) %collective-permute-start.19) | collective-permute-done | bytes 335904 | tf_op jit(solution)/shard_map/ppermute | solution.py:50
  101.1 2.8 %collective-permute-start.20 = (bf16[176,256]{1,0:T(8,128)(2,1)S(1)}, bf16[176,256]{1,0:T(8,128)(2,1)S(1)}, u32[]{:S(2)}, u32[]{:S(2)}) collective-permute-start(bf16[176,256]{1,0:T(8,128)(2,1)S(1)} %get-tuple-element.126), channel_id=1, source_target_pairs={{0,192},{1,193},{2,194},{3,195},{4,196},{5,197},{6,198},{7,199},{8... | collective-permute-start | bytes 270344 | tf_op jit(solution)/shard_map/ppermute | solution.py:46
  103.9 3.5 %collective-permute-start.21 = (bf16[176,256]{1,0:T(8,128)(2,1)S(1)}, bf16[176,256]{1,0:T(8,128)(2,1)S(1)}, u32[]{:S(2)}, u32[]{:S(2)}) collective-permute-start(bf16[176,256]{1,0:T(8,128)(2,1)S(1)} %get-tuple-element.127), channel_id=1, source_target_pairs={{0,240},{1,241},{2,242},{3,243},{4,244},{5,245},{6,246},{7,247},{8... | collective-permute-start | bytes 270344 | tf_op jit(solution)/shard_map/ppermute | solution.py:46
  107.7 3.2 %fusion.2 = bf16[1,512,2048]{2,1,0:T(8,128)(2,1)} fusion(bf16[640,512]{1,0:T(8,128)(2,1)S(1)} %copy-done.7, bf16[640,2048]{1,0:T(8,128)(2,1)S(1)} %copy-done.6), kind=kOutput, calls=%fused_computation.5 | convolution fusion | flops 1343225856 | bytes 5373952 | tf_op jit(solution)/shard_map/dot_general | solution.py:62
  110.8 3.0 %collective-permute-done.23.refs_3_ = bf16[176,256]{1,0:T(8,128)(2,1)S(1)} collective-permute-done((bf16[176,256]{1,0:T(8,128)(2,1)S(1)}, bf16[176,256]{1,0:T(8,128)(2,1)S(1)}, u32[]{:S(2)}, u32[]{:S(2)}) %collective-permute-start.23) | collective-permute-done | bytes 90144 | tf_op jit(solution)/shard_map/ppermute | solution.py:46
  113.8 2.1 %collective-permute-done.22.refs_2_ = bf16[176,256]{1,0:T(8,128)(2,1)S(1)} collective-permute-done((bf16[176,256]{1,0:T(8,128)(2,1)S(1)}, bf16[176,256]{1,0:T(8,128)(2,1)S(1)}, u32[]{:S(2)}, u32[]{:S(2)}) %collective-permute-start.22) | collective-permute-done | bytes 90144 | tf_op jit(solution)/shard_map/ppermute | solution.py:46
  117.4 2.8 %collective-permute-done.24.got = bf16[272,256]{1,0:T(8,128)(2,1)S(1)} collective-permute-done((bf16[272,256]{1,0:T(8,128)(2,1)S(1)}, bf16[272,256]{1,0:T(8,128)(2,1)S(1)}, u32[]{:S(2)}, u32[]{:S(2)}) %collective-permute-start.24) | collective-permute-done | bytes 139296 | tf_op jit(solution)/shard_map/ppermute | solution.py:54
  120.9 4.1 %collective-permute-start.25 = (bf16[128,256]{1,0:T(8,128)(2,1)S(1)}, bf16[128,256]{1,0:T(8,128)(2,1)S(1)}, u32[]{:S(2)}, u32[]{:S(2)}) collective-permute-start(bf16[128,256]{1,0:T(8,128)(2,1)S(1)} %get-tuple-element.140), channel_id=1, source_target_pairs={{0,8},{8,0},{16,24},{24,16},{32,40},{40,32},{48,56},{56,48},{1,9},... | collective-permute-start | bytes 196616 | tf_op jit(solution)/shard_map/ppermute | solution.py:29
  126.0 2.6 %collective-permute-done.29 = f32[8,128]{1,0:T(8,128)S(1)} collective-permute-done((f32[8,128]{1,0:T(8,128)S(1)}, f32[8,128]{1,0:T(8,128)S(1)}, u32[]{:S(2)}, u32[]{:S(2)}) %collective-permute-start.29) | collective-permute-done | bytes 4128 | tf_op jit(solution)/shard_map/ppermute | solution.py:58
  130.8 3.2 %collective-permute-done.27 = bf16[128,512]{1,0:T(8,128)(2,1)S(1)} collective-permute-done((bf16[128,512]{1,0:T(8,128)(2,1)S(1)}, bf16[128,512]{1,0:T(8,128)(2,1)S(1)}, u32[]{:S(2)}, u32[]{:S(2)}) %collective-permute-start.27) | collective-permute-done | bytes 131104 | tf_op jit(solution)/shard_map/ppermute | solution.py:50
  134.0 3.5 %collective-permute-done.28 = bf16[128,512]{1,0:T(8,128)(2,1)S(1)} collective-permute-done((bf16[128,512]{1,0:T(8,128)(2,1)S(1)}, bf16[128,512]{1,0:T(8,128)(2,1)S(1)}, u32[]{:S(2)}, u32[]{:S(2)}) %collective-permute-start.28) | collective-permute-done | bytes 131104 | tf_op jit(solution)/shard_map/ppermute | solution.py:50
  (99 shorter events, 23.1 us)
Async XLA Ops:
  3.0 1.8 %collective-permute-start = (bf16[144,512]{1,0:T(8,128)(2,1)S(1)}, bf16[144,512]{1,0:T(8,128)(2,1)S(1)}, u32[]{:S(2)}, u32[]{:S(2)}) collective-permute-start(bf16[144,512]{1,0:T(8,128)(2,1)S(1)} %get-tuple-element.155), channel_id=1, source_target_pairs={{0,8},{8,0},{16,24},{24,16},{32,40},{40,32},{48,56},{56,48},{1,9},... | collective-permute-start | bytes 442376 | tf_op jit(solution)/shard_map/ppermute | solution.py:29
  6.0 17.0 %collective-permute-start.1 = (bf16[336,256]{1,0:T(8,128)(2,1)S(1)}, bf16[336,256]{1,0:T(8,128)(2,1)S(1)}, u32[]{:S(2)}, u32[]{:S(2)}) collective-permute-start(bf16[336,256]{1,0:T(8,128)(2,1)S(1)} %get-tuple-element.75), channel_id=1, source_target_pairs={{0,16},{8,24},{16,32},{24,40},{32,48},{40,56},{48,0},{56,8},{1,17}... | collective-permute-start | bytes 516104 | tf_op jit(solution)/shard_map/ppermute | solution.py:34
  9.1 16.9 %collective-permute-start.2 = (bf16[336,256]{1,0:T(8,128)(2,1)S(1)}, bf16[336,256]{1,0:T(8,128)(2,1)S(1)}, u32[]{:S(2)}, u32[]{:S(2)}) collective-permute-start(bf16[336,256]{1,0:T(8,128)(2,1)S(1)} %get-tuple-element.76), channel_id=1, source_target_pairs={{0,36},{1,37},{2,38},{3,39},{4,32},{5,33},{6,34},{7,35},{8,44},{9,... | collective-permute-start | bytes 516104 | tf_op jit(solution)/shard_map/ppermute | solution.py:36
  13.8 15.3 %collective-permute-start.3 = (bf16[336,256]{1,0:T(8,128)(2,1)S(1)}, bf16[336,256]{1,0:T(8,128)(2,1)S(1)}, u32[]{:S(2)}, u32[]{:S(2)}) collective-permute-start(bf16[336,256]{1,0:T(8,128)(2,1)S(1)} %get-tuple-element.77), channel_id=1, source_target_pairs={{0,48},{8,56},{16,0},{24,8},{32,16},{40,24},{48,32},{56,40},{1,49}... | collective-permute-start | bytes 516104 | tf_op jit(solution)/shard_map/ppermute | solution.py:34
  20.3 38.7 %copy-start = (bf16[1,512,2048]{2,1,0:T(8,128)(2,1)S(1)}, bf16[1,512,2048]{2,1,0:T(8,128)(2,1)}, u32[]{:S(2)}) copy-start(bf16[1,512,2048]{2,1,0:T(8,128)(2,1)} %param.11) | copy-start | bytes 6291460
  29.1 13.9 %collective-permute-start.5 = (bf16[2,1024,256]{2,1,0:T(8,128)(2,1)}, bf16[2,1024,256]{2,1,0:T(8,128)(2,1)S(1)}, u32[]{:S(2)}, u32[]{:S(2)}) collective-permute-start(bf16[2,1024,256]{2,1,0:T(8,128)(2,1)} %get-tuple-element.83), channel_id=1, source_target_pairs={{0,8},{8,0},{16,24},{24,16},{32,40},{40,32},{48,56},{56,48},{1,9},... | collective-permute-start | bytes 3145736 | tf_op jit(solution)/shard_map/ppermute | solution.py:29
  30.2 12.7 %collective-permute-start.6 = (bf16[2,1024,256]{2,1,0:T(8,128)(2,1)}, bf16[2,1024,256]{2,1,0:T(8,128)(2,1)S(1)}, u32[]{:S(2)}, u32[]{:S(2)}) collective-permute-start(bf16[2,1024,256]{2,1,0:T(8,128)(2,1)} %get-tuple-element.84), channel_id=1, source_target_pairs={{0,8},{8,0},{16,24},{24,16},{32,40},{40,32},{48,56},{56,48},{1,9},... | collective-permute-start | bytes 3145736 | tf_op jit(solution)/shard_map/ppermute | solution.py:29
  30.4 28.6 %copy-start.11 = (bf16[960,256]{1,0:T(8,128)(2,1)}, bf16[960,256]{1,0:T(8,128)(2,1)S(1)}, u32[]{:S(2)}) copy-start(bf16[960,256]{1,0:T(8,128)(2,1)S(1)} %slice_dynamic-update-slice_fusion.refs_0_) | copy-start | bytes 1474564
  30.4 12.6 %collective-permute-start.4 = (bf16[960,256]{1,0:T(8,128)(2,1)S(1)}, bf16[960,256]{1,0:T(8,128)(2,1)}, u32[]{:S(2)}, u32[]{:S(2)}) collective-permute-start(bf16[960,256]{1,0:T(8,128)(2,1)S(1)} %slice_dynamic-update-slice_fusion.refs_0_), channel_id=1, source_target_pairs={{0,1},{1,2},{2,3},{3,0},{4,5},{5,6},{6,7},{7,4},{8,9},{9,10},{10,1... | collective-permute-start | bytes 1474568 | tf_op jit(solution)/shard_map/ppermute | solution.py:50
  30.7 17.5 %collective-permute-start.7 = (bf16[960,256]{1,0:T(8,128)(2,1)S(1)}, bf16[960,256]{1,0:T(8,128)(2,1)}, u32[]{:S(2)}, u32[]{:S(2)}) collective-permute-start(bf16[960,256]{1,0:T(8,128)(2,1)S(1)} %slice_dynamic-update-slice_fusion.refs_0_), channel_id=1, source_target_pairs={{0,2},{1,3},{2,0},{3,1},{4,6},{5,7},{6,4},{7,5},{8,10},{9,11},{10,... | collective-permute-start | bytes 1474568 | tf_op jit(solution)/shard_map/ppermute | solution.py:50
  32.8 23.1 %collective-permute-start.8 = (bf16[960,256]{1,0:T(8,128)(2,1)S(1)}, bf16[960,256]{1,0:T(8,128)(2,1)}, u32[]{:S(2)}, u32[]{:S(2)}) collective-permute-start(bf16[960,256]{1,0:T(8,128)(2,1)S(1)} %slice_dynamic-update-slice_fusion.refs_0_), channel_id=1, source_target_pairs={{0,3},{1,0},{2,1},{3,2},{4,7},{5,4},{6,5},{7,6},{8,11},{9,8},{10,9... | collective-permute-start | bytes 1474568 | tf_op jit(solution)/shard_map/ppermute | solution.py:50
  43.0 13.0 %collective-permute-start.9 = (bf16[1152,128]{1,0:T(8,128)(2,1)S(1)}, bf16[1152,128]{1,0:T(8,128)(2,1)S(1)}, u32[]{:S(2)}, u32[]{:S(2)}) collective-permute-start(bf16[1152,128]{1,0:T(8,128)(2,1)S(1)} %get-tuple-element.88), channel_id=1, source_target_pairs={{0,192},{64,0},{128,64},{192,128},{1,193},{65,1},{129,65},{193,129... | collective-permute-start | bytes 884744 | tf_op jit(solution)/shard_map/ppermute | solution.py:58
  45.8 13.2 %collective-permute-start.14 = (bf16[2,80,2048]{2,1,0:T(8,128)(2,1)}, bf16[2,80,2048]{2,1,0:T(8,128)(2,1)}, u32[]{:S(2)}, u32[]{:S(2)}) collective-permute-start(bf16[2,80,2048]{2,1,0:T(8,128)(2,1)} %local_slots.1.refs_8_), channel_id=1, source_target_pairs={{0,8},{8,0},{16,24},{24,16},{32,40},{40,32},{48,56},{56,48},{1,9},... | collective-permute-start | bytes 1966088 | tf_op jit(solution)/shard_map/ppermute | solution.py:29
  48.2 8.5 %collective-permute-start.10 = (bf16[960,256]{1,0:T(8,128)(2,1)S(1)}, bf16[960,256]{1,0:T(8,128)(2,1)}, u32[]{:S(2)}, u32[]{:S(2)}) collective-permute-start(bf16[960,256]{1,0:T(8,128)(2,1)S(1)} %slice_dynamic-update-slice_fusion.refs_0_), channel_id=1, source_target_pairs={{0,8},{8,0},{16,24},{24,16},{32,40},{40,32},{48,56},{56,48},{1,9},... | collective-permute-start | bytes 1474568 | tf_op jit(solution)/shard_map/ppermute | solution.py:29
  48.2 8.5 %collective-permute-start.11 = (bf16[960,256]{1,0:T(8,128)(2,1)}, bf16[960,256]{1,0:T(8,128)(2,1)}, u32[]{:S(2)}, u32[]{:S(2)}) collective-permute-start(bf16[960,256]{1,0:T(8,128)(2,1)} %collective-permute-done.4.refs_1_), channel_id=1, source_target_pairs={{0,8},{8,0},{16,24},{24,16},{32,40},{40,32},{48,56},{56,48},{1,9},... | collective-permute-start | bytes 1474568 | tf_op jit(solution)/shard_map/ppermute | solution.py:29
  56.0 2.3 %collective-permute-start.12 = (bf16[960,256]{1,0:T(8,128)(2,1)}, bf16[960,256]{1,0:T(8,128)(2,1)}, u32[]{:S(2)}, u32[]{:S(2)}) collective-permute-start(bf16[960,256]{1,0:T(8,128)(2,1)} %collective-permute-done.7.refs_2_), channel_id=1, source_target_pairs={{0,8},{8,0},{16,24},{24,16},{32,40},{40,32},{48,56},{56,48},{1,9},... | collective-permute-start | bytes 1474568 | tf_op jit(solution)/shard_map/ppermute | solution.py:29
  56.5 2.5 %collective-permute-start.13 = (bf16[960,256]{1,0:T(8,128)(2,1)}, bf16[960,256]{1,0:T(8,128)(2,1)}, u32[]{:S(2)}, u32[]{:S(2)}) collective-permute-start(bf16[960,256]{1,0:T(8,128)(2,1)} %collective-permute-done.8.refs_3_), channel_id=1, source_target_pairs={{0,8},{8,0},{16,24},{24,16},{32,40},{40,32},{48,56},{56,48},{1,9},... | collective-permute-start | bytes 1474568 | tf_op jit(solution)/shard_map/ppermute | solution.py:29
  72.3 3.3 %collective-permute-start.15 = (bf16[640,1024]{1,0:T(8,128)(2,1)}, bf16[640,1024]{1,0:T(8,128)(2,1)S(1)}, u32[]{:S(2)}, u32[]{:S(2)}) collective-permute-start(bf16[640,1024]{1,0:T(8,128)(2,1)} %get-tuple-element.106.grads), channel_id=1, source_target_pairs={{0,8},{8,0},{16,24},{24,16},{32,40},{40,32},{48,56},{56,48},{1,9},... | collective-permute-start | bytes 3932168 | tf_op jit(solution)/shard_map/ppermute | solution.py:29
  73.0 2.4 %collective-permute-start.16 = (f32[8,128]{1,0:T(8,128)S(1)}, f32[8,128]{1,0:T(8,128)S(1)}, u32[]{:S(2)}, u32[]{:S(2)}) collective-permute-start(f32[8,128]{1,0:T(8,128)S(1)} %pad.9.router_a), channel_id=1, source_target_pairs={{0,8},{8,0},{16,24},{24,16},{32,40},{40,32},{48,56},{56,48},{1,9},... | collective-permute-start | bytes 12296 | tf_op jit(solution)/shard_map/ppermute | solution.py:29
  80.2 13.6 %collective-permute-start.17 = (bf16[656,256]{1,0:T(8,128)(2,1)S(1)}, bf16[656,256]{1,0:T(8,128)(2,1)S(1)}, u32[]{:S(2)}, u32[]{:S(2)}) collective-permute-start(bf16[656,256]{1,0:T(8,128)(2,1)S(1)} %get-tuple-element.118), channel_id=1, source_target_pairs={{0,1},{1,2},{2,3},{3,0},{4,5},{5,6},{6,7},{7,4},{8,9},{9,10},{10,1... | collective-permute-start | bytes 1007624 | tf_op jit(solution)/shard_map/ppermute | solution.py:50
  81.7 12.1 %collective-permute-start.18 = (bf16[656,256]{1,0:T(8,128)(2,1)S(1)}, bf16[656,256]{1,0:T(8,128)(2,1)S(1)}, u32[]{:S(2)}, u32[]{:S(2)}) collective-permute-start(bf16[656,256]{1,0:T(8,128)(2,1)S(1)} %get-tuple-element.119), channel_id=1, source_target_pairs={{0,2},{1,3},{2,0},{3,1},{4,6},{5,7},{6,4},{7,5},{8,10},{9,11},{10,... | collective-permute-start | bytes 1007624 | tf_op jit(solution)/shard_map/ppermute | solution.py:50
  87.1 12.7 %collective-permute-start.19 = (bf16[656,256]{1,0:T(8,128)(2,1)S(1)}, bf16[656,256]{1,0:T(8,128)(2,1)S(1)}, u32[]{:S(2)}, u32[]{:S(2)}) collective-permute-start(bf16[656,256]{1,0:T(8,128)(2,1)S(1)} %get-tuple-element.120), channel_id=1, source_target_pairs={{0,3},{1,0},{2,1},{3,2},{4,7},{5,4},{6,5},{7,6},{8,11},{9,8},{10,9... | collective-permute-start | bytes 1007624 | tf_op jit(solution)/shard_map/ppermute | solution.py:50
  101.1 9.8 %collective-permute-start.20 = (bf16[176,256]{1,0:T(8,128)(2,1)S(1)}, bf16[176,256]{1,0:T(8,128)(2,1)S(1)}, u32[]{:S(2)}, u32[]{:S(2)}) collective-permute-start(bf16[176,256]{1,0:T(8,128)(2,1)S(1)} %get-tuple-element.126), channel_id=1, source_target_pairs={{0,192},{1,193},{2,194},{3,195},{4,196},{5,197},{6,198},{7,199},{8... | collective-permute-start | bytes 270344 | tf_op jit(solution)/shard_map/ppermute | solution.py:46
  103.9 7.0 %collective-permute-start.21 = (bf16[176,256]{1,0:T(8,128)(2,1)S(1)}, bf16[176,256]{1,0:T(8,128)(2,1)S(1)}, u32[]{:S(2)}, u32[]{:S(2)}) collective-permute-start(bf16[176,256]{1,0:T(8,128)(2,1)S(1)} %get-tuple-element.127), channel_id=1, source_target_pairs={{0,240},{1,241},{2,242},{3,243},{4,244},{5,245},{6,246},{7,247},{8... | collective-permute-start | bytes 270344 | tf_op jit(solution)/shard_map/ppermute | solution.py:46
  107.4 6.5 %collective-permute-start.23 = (bf16[176,256]{1,0:T(8,128)(2,1)S(1)}, bf16[176,256]{1,0:T(8,128)(2,1)S(1)}, u32[]{:S(2)}, u32[]{:S(2)}) collective-permute-start(bf16[176,256]{1,0:T(8,128)(2,1)S(1)} %get-tuple-element.129), channel_id=1, source_target_pairs={{0,208},{1,209},{2,210},{3,211},{4,212},{5,213},{6,214},{7,215},{8... | collective-permute-start | bytes 270344 | tf_op jit(solution)/shard_map/ppermute | solution.py:46
  107.4 8.6 %collective-permute-start.22 = (bf16[176,256]{1,0:T(8,128)(2,1)S(1)}, bf16[176,256]{1,0:T(8,128)(2,1)S(1)}, u32[]{:S(2)}, u32[]{:S(2)}) collective-permute-start(bf16[176,256]{1,0:T(8,128)(2,1)S(1)} %x_sum.2), channel_id=1, source_target_pairs={{0,228},{1,229},{2,230},{3,231},{4,224},{5,225},{6,226},{7,227},{8... | collective-permute-start | bytes 270344 | tf_op jit(solution)/shard_map/ppermute | solution.py:46
  116.3 4.0 %collective-permute-start.24 = (bf16[272,256]{1,0:T(8,128)(2,1)S(1)}, bf16[272,256]{1,0:T(8,128)(2,1)S(1)}, u32[]{:S(2)}, u32[]{:S(2)}) collective-permute-start(bf16[272,256]{1,0:T(8,128)(2,1)S(1)} %return_slots.1.partial), channel_id=1, source_target_pairs={{0,4},{1,5},{2,6},{3,7},{4,0},{5,1},{6,2},{7,3},{8,12},{9,13},{10,... | collective-permute-start | bytes 417800 | tf_op jit(solution)/shard_map/ppermute | solution.py:54
  120.9 5.0 %collective-permute-start.25 = (bf16[128,256]{1,0:T(8,128)(2,1)S(1)}, bf16[128,256]{1,0:T(8,128)(2,1)S(1)}, u32[]{:S(2)}, u32[]{:S(2)}) collective-permute-start(bf16[128,256]{1,0:T(8,128)(2,1)S(1)} %get-tuple-element.140), channel_id=1, source_target_pairs={{0,8},{8,0},{16,24},{24,16},{32,40},{40,32},{48,56},{56,48},{1,9},... | collective-permute-start | bytes 196616 | tf_op jit(solution)/shard_map/ppermute | solution.py:29
  124.9 3.7 %collective-permute-start.29 = (f32[8,128]{1,0:T(8,128)S(1)}, f32[8,128]{1,0:T(8,128)S(1)}, u32[]{:S(2)}, u32[]{:S(2)}) collective-permute-start(f32[8,128]{1,0:T(8,128)S(1)} %get-tuple-element.141), channel_id=1, source_target_pairs={{0,64},{64,128},{128,192},{192,0},{1,65},{65,129},{129,193},{193,1... | collective-permute-start | bytes 12296 | tf_op jit(solution)/shard_map/ppermute | solution.py:58
  125.9 4.8 %collective-permute-start.26 = (bf16[128,512]{1,0:T(8,128)(2,1)S(1)}, bf16[128,512]{1,0:T(8,128)(2,1)S(1)}, u32[]{:S(2)}, u32[]{:S(2)}) collective-permute-start(bf16[128,512]{1,0:T(8,128)(2,1)S(1)} %get-tuple-element.151), channel_id=1, source_target_pairs={{0,1},{1,2},{2,3},{3,0},{4,5},{5,6},{6,7},{7,4},{8,9},{9,10},{10,1... | collective-permute-start | bytes 393224 | tf_op jit(solution)/shard_map/ppermute | solution.py:50
  128.6 5.3 %collective-permute-start.27 = (bf16[128,512]{1,0:T(8,128)(2,1)S(1)}, bf16[128,512]{1,0:T(8,128)(2,1)S(1)}, u32[]{:S(2)}, u32[]{:S(2)}) collective-permute-start(bf16[128,512]{1,0:T(8,128)(2,1)S(1)} %get-tuple-element.151), channel_id=1, source_target_pairs={{0,2},{1,3},{2,0},{3,1},{4,6},{5,7},{6,4},{7,5},{8,10},{9,11},{10,... | collective-permute-start | bytes 393224 | tf_op jit(solution)/shard_map/ppermute | solution.py:50
  130.5 6.9 %collective-permute-start.28 = (bf16[128,512]{1,0:T(8,128)(2,1)S(1)}, bf16[128,512]{1,0:T(8,128)(2,1)S(1)}, u32[]{:S(2)}, u32[]{:S(2)}) collective-permute-start(bf16[128,512]{1,0:T(8,128)(2,1)S(1)} %get-tuple-element.151), channel_id=1, source_target_pairs={{0,3},{1,0},{2,1},{3,2},{4,7},{5,4},{6,5},{7,6},{8,11},{9,8},{10,9... | collective-permute-start | bytes 393224 | tf_op jit(solution)/shard_map/ppermute | solution.py:50
  (12 other events, 85.6 us)

commit v2 on v1

--- a/solution.py
+++ b/solution.py
@@ -195,26 +195,32 @@
 
 def expert_kernel(where_ref, *refs):
     pieces, local = refs[:8], refs[8:10]
-    gate_rows, up_rows, down_rows, gates_ref = refs[10:14]
+    up_hbm, down_hbm, gate_rows, gates_ref = refs[10:14]
     input_out, grad_out, gpg_out, upg_out, scaled_out, router, grads = refs[14:21]
-    inputs, out_grads, scaled, sems = refs[21:]
+    inputs, out_grads, scaled, up_rows, down_rows, pre_gate, sems = refs[21:]
+    wait_all(copy_all(gather_rows(where_ref, pieces, local, 0, inputs), sems))
     loads = copy_all(
-        gather_rows(where_ref, pieces, local, 0, inputs)
-        + gather_rows(where_ref, pieces, local, 1, out_grads),
+        [(up_hbm, up_rows)]
+        + gather_rows(where_ref, pieces, local, 1, out_grads)
+        + [(down_hbm, down_rows)],
         sems,
+        10,
     )
-    wait_all(loads[:10])
-    stores = copy_all([(inputs, input_out)], sems, 20)
+    stores = copy_all([(inputs, input_out)], sems, 22)
+    for n in range(2):
+        units = slice(n * 256, n * 256 + 256)
+        pre_gate[:, units] = dot(inputs[...], gate_rows[units, :], ((1,), (1,)))
+    loads[0].wait()
     gates = gates_ref[...]
     router_sum = jnp.zeros((ROWS, 1), F32)
     for n in range(2):
         units = slice(n * 256, n * 256 + 256)
         ups = slice(UNITS + n * 256, UNITS + n * 256 + 256)
-        v = dot(inputs[...], gate_rows[units, :], ((1,), (1,)))
+        v = pre_gate[:, units]
         up = dot(inputs[...], up_rows[units, :], ((1,), (1,)))
         if n == 0:
-            wait_all(loads[10:])
-            stores += copy_all([(out_grads, grad_out)], sems, 21)
+            wait_all(loads[1:])
+            stores += copy_all([(out_grads, grad_out)], sems, 23)
         hidden_grad = dot(out_grads[...], down_rows[units, :], ((1,), (1,)))
         s = jax.nn.sigmoid(v)
         activated = v * s
@@ -231,7 +237,7 @@
                 (scaled.at[:, units], scaled_out.at[:, units]),
             ],
             sems,
-            22 + 3 * n,
+            24 + 3 * n,
         )
     router[...] = router_sum
     wait_all(stores)
@@ -249,18 +255,21 @@
             jax.ShapeDtypeStruct((ROWS, 1), F32),
             jax.ShapeDtypeStruct((ROWS, 2 * UNITS), BF),
         ],
-        in_specs=[SMEM] + [ANY] * 10 + [VMEM] * 4,
+        in_specs=[SMEM] + [ANY] * 12 + [VMEM] * 2,
         out_specs=[ANY] * 5 + [VMEM] * 2,
         scratch_shapes=[
             pltpu.VMEM((ROWS, D), BF),
             pltpu.VMEM((ROWS, D), BF),
             pltpu.VMEM((ROWS, UNITS), BF),
-            pltpu.SemaphoreType.DMA((28,)),
+            pltpu.VMEM((UNITS, D), BF),
+            pltpu.VMEM((UNITS, D), BF),
+            pltpu.VMEM((ROWS, UNITS), F32),
+            pltpu.SemaphoreType.DMA((30,)),
         ],
-        compiler_params=params(16),
+        compiler_params=params(20),
         cost_estimate=cost(3 * 2 * ROWS * D * UNITS, 12_000_000),
         name="expert_work",
-    )(where, *map(pinned, pieces), *map(pinned, local), w_gate, w_up, w_down, gates)
+    )(where, *map(pinned, pieces), *map(pinned, local), w_up, w_down, w_gate, gates)
 
 
 CHUNKS = ((2, 1), (3, 0))
@@ -485,7 +494,7 @@
     own, near, given, pack = lax.optimization_barrier((pieces[0], pieces[1], given, pack))
     pack = section_shift(pack, -1)
     given = [pinned(g) for g in given]
-    pieces[2], pieces[3], pack = lax.optimization_barrier((pieces[2], pieces[3], pack))
+    pieces[2], pack = lax.optimization_barrier((pieces[2], pack))
     pieces[:2] = own, near
     gates = jnp.stack([gate0[:2, :CAP]] + [z[2 * PAIR : 2 * PAIR + 2, :CAP] for z in away])
     gates = gates.astype(F32).reshape(ROWS, 1)
@@ -493,7 +502,7 @@
     pieces, given = lax.optimization_barrier((pieces, given))
 
     rows_input, rows_grad, gpg, upg, scaled, router, half = expert_work(
-        where, pieces, local, w_gate[0], w_up[0], w_down[0], gates
+        where, pieces, local, w_gate[0], up_rows, pinned(w_down[0]), gates
     )
     got = core_swap(half)
     router = jnp.pad(router.reshape(8, CAP), ((0, 0), (0, TOK - CAP)))

time: 140 us -> 139 us (level)
  starting transfers between devices: 37.7 us -> 42.3 us
  waiting for transfers between devices: 53.3 us -> 49.1 us
  local copies, waits for them, and re-layouts: 7.79 us -> 4.61 us
  Pallas kernels: 26.8 us -> 29.1 us
    ppermute x11, starting transfers between devices: 10.2 us -> 17 us  [core_swap(): return lax.ppermute(a, 'expert', [(i, i ^ 1) for i in range(8)])]
    ppermute x9, waiting for transfers between devices: 30.4 us -> 24.4 us  [x_shift(): lax.ppermute(a, 'dp', [(i, i // 4 * 4 + (i + j) % 4) for i in range(8)])]
    unnamed x33 -> x29, local copies, waits for them, and re-layouts: 6.49 us -> 3.31 us
    pallas_call x1, Pallas kernels: 10.1 us -> 12.4 us  [expert_work(): pl.pallas_call(expert_kernel, out_shape=[pltpu.HBM((ROWS, D), BF), pltpu....]
    ppermute x9, starting transfers between devices: 6.68 us -> 4.69 us  [x_shift(): lax.ppermute(a, 'dp', [(i, i // 4 * 4 + (i + j) % 4) for i in range(8)])]
  transfers between devices with their start and end apart: 30 -> 30, of which waited for: 18 -> 19; matrix products, arithmetic and copies ran while one was open for 8% -> 8% of each run, Pallas kernels for 7% -> 7%
where the time goes in v2:
time: 139 us; the launch traced here: 138 us
  waiting for transfers between devices  49.1 us (35%)
  starting transfers between devices  42.3 us (30%)
  Pallas kernels  29.1 us (21%)
  matrix products  9.44 us (7%)
  local copies, waits for them, and re-layouts  4.61 us (3%)
  other arithmetic  2.27 us (2%)
    ppermute x9, waiting for transfers between devices, x_shift(): lax.ppermute(a, 'dp', [(i, i // 4 * 4 + (i + j) % 4) for i in range(8)])  24.4 us
    ppermute x11, starting transfers between devices, core_swap(): return lax.ppermute(a, 'expert', [(i, i ^ 1) for i in range(8)])  17 us
    pallas_call x1, Pallas kernels, expert_work(): pl.pallas_call(expert_kernel, out_shape=[pltpu.HBM((ROWS, D), BF), pltpu....  12.4 us
    dot_general x3, matrix products, dot(): return lax.dot_general(a, b, (dims, ((), ())), preferred_element_type=F32)  9.44 us
    ppermute x11, waiting for transfers between devices, core_swap(): return lax.ppermute(a, 'expert', [(i, i ^ 1) for i in range(8)])  7.07 us
    ppermute x4, starting transfers between devices, chip_return(): return lax.ppermute(a, ('section', 'expert', 'dp'), route)  6.59 us
    pallas_call x2, Pallas kernels, part_work(): pl.pallas_call(functools.partial(part_kernel, chunks), out_shape=shapes,...  6.42 us
    ppermute x4, waiting for transfers between devices, chip_return(): return lax.ppermute(a, ('section', 'expert', 'dp'), route)  6.02 us
  transfers between devices with their start and end apart: 30, of which 19 were waited for; matrix products, arithmetic and copies ran while one was open for 8% of the time, Pallas kernels for 7%

profile of v2, /device:TPU:7, one launch (start us, length us, event | category | flops | bytes accessed | tf_op | source)
XLA Modules:
  0.0 137.8 jit_solution(296918487103643)
XLA Ops:
  6.0 3.1 %collective-permute-start.1 = (bf16[336,256]{1,0:T(8,128)(2,1)S(1)}, bf16[336,256]{1,0:T(8,128)(2,1)S(1)}, u32[]{:S(2)}, u32[]{:S(2)}) collective-permute-start(bf16[336,256]{1,0:T(8,128)(2,1)S(1)} %get-tuple-element.74), channel_id=1, source_target_pairs={{0,16},{8,24},{16,32},{24,40},{32,48},{40,56},{48,0},{56,8},{1,17}... | collective-permute-start | bytes 516104 | tf_op jit(solution)/shard_map/ppermute | solution.py:34
  9.1 4.7 %collective-permute-start.2 = (bf16[336,256]{1,0:T(8,128)(2,1)S(1)}, bf16[336,256]{1,0:T(8,128)(2,1)S(1)}, u32[]{:S(2)}, u32[]{:S(2)}) collective-permute-start(bf16[336,256]{1,0:T(8,128)(2,1)S(1)} %get-tuple-element.75), channel_id=1, source_target_pairs={{0,36},{1,37},{2,38},{3,39},{4,32},{5,33},{6,34},{7,35},{8,44},{9,... | collective-permute-start | bytes 516104 | tf_op jit(solution)/shard_map/ppermute | solution.py:36
  13.8 2.4 %collective-permute-start.3 = (bf16[336,256]{1,0:T(8,128)(2,1)S(1)}, bf16[336,256]{1,0:T(8,128)(2,1)S(1)}, u32[]{:S(2)}, u32[]{:S(2)}) collective-permute-start(bf16[336,256]{1,0:T(8,128)(2,1)S(1)} %get-tuple-element.76), channel_id=1, source_target_pairs={{0,48},{8,56},{16,0},{24,8},{32,16},{40,24},{48,32},{56,40},{1,49}... | collective-permute-start | bytes 516104 | tf_op jit(solution)/shard_map/ppermute | solution.py:34
  16.1 4.2 %arrange_weights.1 = (bf16[2,1024,256]{2,1,0:T(8,128)(2,1)}, bf16[2,1024,256]{2,1,0:T(8,128)(2,1)}, bf16[2,1024,256]{2,1,0:T(8,128)(2,1)}, bf16[2,1024,256]{2,1,0:T(8,128)(2,1)}) custom-call(s32[2]{0:T(128)S(1)} %pad_add_fusion.where_ref, bf16[512,2048]{1,0:T(8,128)(2,1)} %bitcast.30, bf16[512,2048]{1,0:T(8,128)(2,1)} %bitcast.32), custom_call_target="tpu_custom_call" | custom-call | bytes 8000000 | tf_op jit(solution)/shard_map/arrange_weights/pallas_call | solution.py:298
  20.3 2.7 %local_slots.1.refs_8_ = bf16[2,80,2048]{2,1,0:T(8,128)(2,1)} custom-call(bf16[144,512]{1,0:T(8,128)(2,1)S(1)} %get-tuple-element.154.mine_ref, bf16[128,2048]{1,0:T(8,128)(2,1)} %input_ref.1, bf16[128,2048]{1,0:T(8,128)(2,1)} %grad_ref.1), custom_call_target="tpu_custom_call" | custom-call | flops 100000000 | bytes 2000000 | tf_op jit(solution)/shard_map/local_slots/pallas_call | solution.py:150
  23.0 3.0 %collective-permute-done.2 = bf16[336,256]{1,0:T(8,128)(2,1)S(1)} collective-permute-done((bf16[336,256]{1,0:T(8,128)(2,1)S(1)}, bf16[336,256]{1,0:T(8,128)(2,1)S(1)}, u32[]{:S(2)}, u32[]{:S(2)}) %collective-permute-start.2) | collective-permute-done | bytes 172064 | tf_op jit(solution)/shard_map/ppermute | solution.py:36
  26.0 3.0 %collective-permute-done.3 = bf16[336,256]{1,0:T(8,128)(2,1)S(1)} collective-permute-done((bf16[336,256]{1,0:T(8,128)(2,1)S(1)}, bf16[336,256]{1,0:T(8,128)(2,1)S(1)}, u32[]{:S(2)}, u32[]{:S(2)}) %collective-permute-start.3) | collective-permute-done | bytes 172064 | tf_op jit(solution)/shard_map/ppermute | solution.py:34
  30.7 1.3 collective-permute-start.9
  33.1 9.9 %collective-permute-done.4.refs_1_ = bf16[960,256]{1,0:T(8,128)(2,1)} collective-permute-done((bf16[960,256]{1,0:T(8,128)(2,1)S(1)}, bf16[960,256]{1,0:T(8,128)(2,1)}, u32[]{:S(2)}, u32[]{:S(2)}) %collective-permute-start.4) | collective-permute-done | bytes 491552 | tf_op jit(solution)/shard_map/ppermute | solution.py:50
  43.0 2.8 %collective-permute-start.8 = (bf16[1152,128]{1,0:T(8,128)(2,1)S(1)}, bf16[1152,128]{1,0:T(8,128)(2,1)S(1)}, u32[]{:S(2)}, u32[]{:S(2)}) collective-permute-start(bf16[1152,128]{1,0:T(8,128)(2,1)S(1)} %get-tuple-element.87), channel_id=1, source_target_pairs={{0,192},{64,0},{128,64},{192,128},{1,193},{65,1},{129,65},{193,129... | collective-permute-start | bytes 884744 | tf_op jit(solution)/shard_map/ppermute | solution.py:58
  45.8 2.4 %collective-permute-start.14 = (bf16[2,80,2048]{2,1,0:T(8,128)(2,1)}, bf16[2,80,2048]{2,1,0:T(8,128)(2,1)}, u32[]{:S(2)}, u32[]{:S(2)}) collective-permute-start(bf16[2,80,2048]{2,1,0:T(8,128)(2,1)} %local_slots.1.refs_8_), channel_id=1, source_target_pairs={{0,8},{8,0},{16,24},{24,16},{32,40},{40,32},{48,56},{56,48},{1,9},... | collective-permute-start | bytes 1966088 | tf_op jit(solution)/shard_map/ppermute | solution.py:29
  48.2 8.0 %collective-permute-start.13 = (bf16[960,256]{1,0:T(8,128)(2,1)}, bf16[960,256]{1,0:T(8,128)(2,1)}, u32[]{:S(2)}, u32[]{:S(2)}) collective-permute-start(bf16[960,256]{1,0:T(8,128)(2,1)} %collective-permute-done.9.refs_3_), channel_id=1, source_target_pairs={{0,8},{8,0},{16,24},{24,16},{32,40},{40,32},{48,56},{56,48},{1,9},... | collective-permute-start | bytes 1474568 | tf_op jit(solution)/shard_map/ppermute | solution.py:29
  57.2 1.5 %collective-permute-done.13.refs_7_ = bf16[960,256]{1,0:T(8,128)(2,1)} collective-permute-done((bf16[960,256]{1,0:T(8,128)(2,1)}, bf16[960,256]{1,0:T(8,128)(2,1)}, u32[]{:S(2)}, u32[]{:S(2)}) %collective-permute-start.13) | collective-permute-done | bytes 491552 | tf_op jit(solution)/shard_map/ppermute | solution.py:29
  60.1 12.4 %expert_work.1 = (bf16[640,2048]{1,0:T(8,128)(2,1)}, bf16[640,2048]{1,0:T(8,128)(2,1)}, bf16[640,512]{1,0:T(8,128)(2,1)}, bf16[640,512]{1,0:T(8,128)(2,1)}, bf16...) custom-call(s32[2]{0:T(128)S(1)} %pad_add_fusion.where_ref, bf16[960,256]{1,0:T(8,128)(2,1)} %copy-done.9, ...), custom_call_target="tpu_custom_call" | custom-call | flops 4026531840 | bytes 12000000 | tf_op jit(solution)/shard_map/expert_work/pallas_call | solution.py:247
  73.5 2.2 %collective-permute-done.16.router_b = f32[8,128]{1,0:T(8,128)S(1)} collective-permute-done((f32[8,128]{1,0:T(8,128)S(1)}, f32[8,128]{1,0:T(8,128)S(1)}, u32[]{:S(2)}, u32[]{:S(2)}) %collective-permute-start.16) | collective-permute-done | bytes 4128 | tf_op jit(solution)/shard_map/ppermute | solution.py:29
  77.1 3.3 %part_work.3 = (bf16[656,256]{1,0:T(8,128)(2,1)S(1)}, bf16[656,256]{1,0:T(8,128)(2,1)S(1)}) custom-call(bf16[640,1024]{1,0:T(8,128)(2,1)} %get-tuple-element.104.grads, bf16[640,1024]{1,0:T(8,128)(2,1)S(1)} %collective-permute-done.15.got, bf16[2,1024,256]{2,1,0:T(8,128)(2,1)S(1)} %copy-done.2, bf16[2,1024,256]{2,1,0:T(8,128)(2,1)} %copy-done.11, ...), custom_call_target="tpu_custom_call" | custom-call | flops 1342177280 | bytes 6000000 | tf_op jit(solution)/shard_map/part_work/pallas_call | solution.py:333
  81.9 3.1 %part_work.2 = (bf16[656,256]{1,0:T(8,128)(2,1)S(1)}, f32[640,256]{1,0:T(8,128)S(1)}) custom-call(bf16[640,1024]{1,0:T(8,128)(2,1)} %get-tuple-element.104.grads, bf16[640,1024]{1,0:T(8,128)(2,1)S(1)} %collective-permute-done.15.got, bf16[2,1024,256]{2,1,0:T(8,128)(2,1)S(1)} %copy-done.1, bf16[2,1024,256]{2,1,0:T(8,128)(2,1)} %copy-done.10, ...), custom_call_target="tpu_custom_call" | custom-call | flops 1342177280 | bytes 6000000 | tf_op jit(solution)/shard_map/part_work/pallas_call | solution.py:333
  85.1 1.5 %collective-permute-start.19 = (bf16[656,256]{1,0:T(8,128)(2,1)S(1)}, bf16[656,256]{1,0:T(8,128)(2,1)S(1)}, u32[]{:S(2)}, u32[]{:S(2)}) collective-permute-start(bf16[656,256]{1,0:T(8,128)(2,1)S(1)} %get-tuple-element.118), channel_id=1, source_target_pairs={{0,3},{1,0},{2,1},{3,2},{4,7},{5,4},{6,5},{7,6},{8,11},{9,8},{10,9... | collective-permute-start | bytes 1007624 | tf_op jit(solution)/shard_map/ppermute | solution.py:50
  86.6 3.1 %fusion.1 = bf16[1,512,2048]{2,1,0:T(8,128)(2,1)} fusion(bf16[640,512]{1,0:T(8,128)(2,1)S(1)} %copy-done.7, bf16[640,2048]{1,0:T(8,128)(2,1)S(1)} %copy-done.3), kind=kOutput, calls=%fused_computation.4 | convolution fusion | flops 1343225856 | bytes 5373952 | tf_op jit(solution)/shard_map/dot_general | solution.py:62
  89.7 3.2 %fusion = bf16[1,512,2048]{2,1,0:T(8,128)(2,1)} fusion(bf16[640,512]{1,0:T(8,128)(2,1)S(1)} %copy-done.6, bf16[640,2048]{1,0:T(8,128)(2,1)S(1)} %copy-done.3), kind=kOutput, calls=%fused_computation.3 | convolution fusion | flops 1343225856 | bytes 5373952 | tf_op jit(solution)/shard_map/dot_general | solution.py:62
  92.9 6.2 %collective-permute-done.19.refs_2_ = bf16[656,256]{1,0:T(8,128)(2,1)S(1)} collective-permute-done((bf16[656,256]{1,0:T(8,128)(2,1)S(1)}, bf16[656,256]{1,0:T(8,128)(2,1)S(1)}, u32[]{:S(2)}, u32[]{:S(2)}) %collective-permute-start.19) | collective-permute-done | bytes 335904 | tf_op jit(solution)/shard_map/ppermute | solution.py:50
  100.3 2.8 %collective-permute-start.20 = (bf16[176,256]{1,0:T(8,128)(2,1)S(1)}, bf16[176,256]{1,0:T(8,128)(2,1)S(1)}, u32[]{:S(2)}, u32[]{:S(2)}) collective-permute-start(bf16[176,256]{1,0:T(8,128)(2,1)S(1)} %get-tuple-element.124), channel_id=1, source_target_pairs={{0,192},{1,193},{2,194},{3,195},{4,196},{5,197},{6,198},{7,199},{8... | collective-permute-start | bytes 270344 | tf_op jit(solution)/shard_map/ppermute | solution.py:46
  103.1 3.5 %collective-permute-start.21 = (bf16[176,256]{1,0:T(8,128)(2,1)S(1)}, bf16[176,256]{1,0:T(8,128)(2,1)S(1)}, u32[]{:S(2)}, u32[]{:S(2)}) collective-permute-start(bf16[176,256]{1,0:T(8,128)(2,1)S(1)} %get-tuple-element.125), channel_id=1, source_target_pairs={{0,240},{1,241},{2,242},{3,243},{4,244},{5,245},{6,246},{7,247},{8... | collective-permute-start | bytes 270344 | tf_op jit(solution)/shard_map/ppermute | solution.py:46
  106.9 3.1 %fusion.2 = bf16[1,512,2048]{2,1,0:T(8,128)(2,1)} fusion(bf16[640,512]{1,0:T(8,128)(2,1)S(1)} %copy-done.5, bf16[640,2048]{1,0:T(8,128)(2,1)S(1)} %copy-done.4), kind=kOutput, calls=%fused_computation.5 | convolution fusion | flops 1343225856 | bytes 5373952 | tf_op jit(solution)/shard_map/dot_general | solution.py:62
  110.1 3.0 %collective-permute-done.23.refs_3_ = bf16[176,256]{1,0:T(8,128)(2,1)S(1)} collective-permute-done((bf16[176,256]{1,0:T(8,128)(2,1)S(1)}, bf16[176,256]{1,0:T(8,128)(2,1)S(1)}, u32[]{:S(2)}, u32[]{:S(2)}) %collective-permute-start.23) | collective-permute-done | bytes 90144 | tf_op jit(solution)/shard_map/ppermute | solution.py:46
  113.1 3.0 %collective-permute-done.22.refs_2_ = bf16[176,256]{1,0:T(8,128)(2,1)S(1)} collective-permute-done((bf16[176,256]{1,0:T(8,128)(2,1)S(1)}, bf16[176,256]{1,0:T(8,128)(2,1)S(1)}, u32[]{:S(2)}, u32[]{:S(2)}) %collective-permute-start.22) | collective-permute-done | bytes 90144 | tf_op jit(solution)/shard_map/ppermute | solution.py:46
  117.4 3.0 %collective-permute-done.24.got = bf16[272,256]{1,0:T(8,128)(2,1)S(1)} collective-permute-done((bf16[272,256]{1,0:T(8,128)(2,1)S(1)}, bf16[272,256]{1,0:T(8,128)(2,1)S(1)}, u32[]{:S(2)}, u32[]{:S(2)}) %collective-permute-start.24) | collective-permute-done | bytes 139296 | tf_op jit(solution)/shard_map/ppermute | solution.py:54
  121.0 3.1 %collective-permute-start.25 = (bf16[128,256]{1,0:T(8,128)(2,1)S(1)}, bf16[128,256]{1,0:T(8,128)(2,1)S(1)}, u32[]{:S(2)}, u32[]{:S(2)}) collective-permute-start(bf16[128,256]{1,0:T(8,128)(2,1)S(1)} %get-tuple-element.138), channel_id=1, source_target_pairs={{0,8},{8,0},{16,24},{24,16},{32,40},{40,32},{48,56},{56,48},{1,9},... | collective-permute-start | bytes 196616 | tf_op jit(solution)/shard_map/ppermute | solution.py:29
  125.3 2.6 %collective-permute-done.29 = f32[8,128]{1,0:T(8,128)S(1)} collective-permute-done((f32[8,128]{1,0:T(8,128)S(1)}, f32[8,128]{1,0:T(8,128)S(1)}, u32[]{:S(2)}, u32[]{:S(2)}) %collective-permute-start.29) | collective-permute-done | bytes 4128 | tf_op jit(solution)/shard_map/ppermute | solution.py:58
  128.5 1.5 %collective-permute-done.26 = bf16[128,512]{1,0:T(8,128)(2,1)S(1)} collective-permute-done((bf16[128,512]{1,0:T(8,128)(2,1)S(1)}, bf16[128,512]{1,0:T(8,128)(2,1)S(1)}, u32[]{:S(2)}, u32[]{:S(2)}) %collective-permute-start.26) | collective-permute-done | bytes 131104 | tf_op jit(solution)/shard_map/ppermute | solution.py:50
  130.0 3.3 %collective-permute-done.27 = bf16[128,512]{1,0:T(8,128)(2,1)S(1)} collective-permute-done((bf16[128,512]{1,0:T(8,128)(2,1)S(1)}, bf16[128,512]{1,0:T(8,128)(2,1)S(1)}, u32[]{:S(2)}, u32[]{:S(2)}) %collective-permute-start.27) | collective-permute-done | bytes 131104 | tf_op jit(solution)/shard_map/ppermute | solution.py:50
  133.3 3.6 %collective-permute-done.28 = bf16[128,512]{1,0:T(8,128)(2,1)S(1)} collective-permute-done((bf16[128,512]{1,0:T(8,128)(2,1)S(1)}, bf16[128,512]{1,0:T(8,128)(2,1)S(1)}, u32[]{:S(2)}, u32[]{:S(2)}) %collective-permute-start.28) | collective-permute-done | bytes 131104 | tf_op jit(solution)/shard_map/ppermute | solution.py:50
  (95 shorter events, 20.5 us)
Async XLA Ops:
  3.0 1.8 %collective-permute-start = (bf16[144,512]{1,0:T(8,128)(2,1)S(1)}, bf16[144,512]{1,0:T(8,128)(2,1)S(1)}, u32[]{:S(2)}, u32[]{:S(2)}) collective-permute-start(bf16[144,512]{1,0:T(8,128)(2,1)S(1)} %get-tuple-element.153), channel_id=1, source_target_pairs={{0,8},{8,0},{16,24},{24,16},{32,40},{40,32},{48,56},{56,48},{1,9},... | collective-permute-start | bytes 442376 | tf_op jit(solution)/shard_map/ppermute | solution.py:29
  6.0 17.0 %collective-permute-start.1 = (bf16[336,256]{1,0:T(8,128)(2,1)S(1)}, bf16[336,256]{1,0:T(8,128)(2,1)S(1)}, u32[]{:S(2)}, u32[]{:S(2)}) collective-permute-start(bf16[336,256]{1,0:T(8,128)(2,1)S(1)} %get-tuple-element.74), channel_id=1, source_target_pairs={{0,16},{8,24},{16,32},{24,40},{32,48},{40,56},{48,0},{56,8},{1,17}... | collective-permute-start | bytes 516104 | tf_op jit(solution)/shard_map/ppermute | solution.py:34
  9.1 16.9 %collective-permute-start.2 = (bf16[336,256]{1,0:T(8,128)(2,1)S(1)}, bf16[336,256]{1,0:T(8,128)(2,1)S(1)}, u32[]{:S(2)}, u32[]{:S(2)}) collective-permute-start(bf16[336,256]{1,0:T(8,128)(2,1)S(1)} %get-tuple-element.75), channel_id=1, source_target_pairs={{0,36},{1,37},{2,38},{3,39},{4,32},{5,33},{6,34},{7,35},{8,44},{9,... | collective-permute-start | bytes 516104 | tf_op jit(solution)/shard_map/ppermute | solution.py:36
  13.8 15.3 %collective-permute-start.3 = (bf16[336,256]{1,0:T(8,128)(2,1)S(1)}, bf16[336,256]{1,0:T(8,128)(2,1)S(1)}, u32[]{:S(2)}, u32[]{:S(2)}) collective-permute-start(bf16[336,256]{1,0:T(8,128)(2,1)S(1)} %get-tuple-element.76), channel_id=1, source_target_pairs={{0,48},{8,56},{16,0},{24,8},{32,16},{40,24},{48,32},{56,40},{1,49}... | collective-permute-start | bytes 516104 | tf_op jit(solution)/shard_map/ppermute | solution.py:34
  20.3 39.8 %copy-start = (bf16[1,512,2048]{2,1,0:T(8,128)(2,1)S(1)}, bf16[1,512,2048]{2,1,0:T(8,128)(2,1)}, u32[]{:S(2)}) copy-start(bf16[1,512,2048]{2,1,0:T(8,128)(2,1)} %param.11) | copy-start | bytes 6291460
  29.1 13.9 %collective-permute-start.5 = (bf16[2,1024,256]{2,1,0:T(8,128)(2,1)}, bf16[2,1024,256]{2,1,0:T(8,128)(2,1)S(1)}, u32[]{:S(2)}, u32[]{:S(2)}) collective-permute-start(bf16[2,1024,256]{2,1,0:T(8,128)(2,1)} %get-tuple-element.82), channel_id=1, source_target_pairs={{0,8},{8,0},{16,24},{24,16},{32,40},{40,32},{48,56},{56,48},{1,9},... | collective-permute-start | bytes 3145736 | tf_op jit(solution)/shard_map/ppermute | solution.py:29
  30.2 12.7 %collective-permute-start.6 = (bf16[2,1024,256]{2,1,0:T(8,128)(2,1)}, bf16[2,1024,256]{2,1,0:T(8,128)(2,1)S(1)}, u32[]{:S(2)}, u32[]{:S(2)}) collective-permute-start(bf16[2,1024,256]{2,1,0:T(8,128)(2,1)} %get-tuple-element.83), channel_id=1, source_target_pairs={{0,8},{8,0},{16,24},{24,16},{32,40},{40,32},{48,56},{56,48},{1,9},... | collective-permute-start | bytes 3145736 | tf_op jit(solution)/shard_map/ppermute | solution.py:29
  30.4 29.7 %copy-start.9 = (bf16[960,256]{1,0:T(8,128)(2,1)}, bf16[960,256]{1,0:T(8,128)(2,1)S(1)}, u32[]{:S(2)}) copy-start(bf16[960,256]{1,0:T(8,128)(2,1)S(1)} %slice_dynamic-update-slice_fusion.refs_0_) | copy-start | bytes 1474564
  30.4 12.6 %collective-permute-start.4 = (bf16[960,256]{1,0:T(8,128)(2,1)S(1)}, bf16[960,256]{1,0:T(8,128)(2,1)}, u32[]{:S(2)}, u32[]{:S(2)}) collective-permute-start(bf16[960,256]{1,0:T(8,128)(2,1)S(1)} %slice_dynamic-update-slice_fusion.refs_0_), channel_id=1, source_target_pairs={{0,1},{1,2},{2,3},{3,0},{4,5},{5,6},{6,7},{7,4},{8,9},{9,10},{10,1... | collective-permute-start | bytes 1474568 | tf_op jit(solution)/shard_map/ppermute | solution.py:50
  30.7 17.5 %collective-permute-start.9 = (bf16[960,256]{1,0:T(8,128)(2,1)S(1)}, bf16[960,256]{1,0:T(8,128)(2,1)}, u32[]{:S(2)}, u32[]{:S(2)}) collective-permute-start(bf16[960,256]{1,0:T(8,128)(2,1)S(1)} %slice_dynamic-update-slice_fusion.refs_0_), channel_id=1, source_target_pairs={{0,3},{1,0},{2,1},{3,2},{4,7},{5,4},{6,5},{7,6},{8,11},{9,8},{10,9... | collective-permute-start | bytes 1474568 | tf_op jit(solution)/shard_map/ppermute | solution.py:50
  32.0 24.2 %collective-permute-start.7 = (bf16[960,256]{1,0:T(8,128)(2,1)S(1)}, bf16[960,256]{1,0:T(8,128)(2,1)}, u32[]{:S(2)}, u32[]{:S(2)}) collective-permute-start(bf16[960,256]{1,0:T(8,128)(2,1)S(1)} %slice_dynamic-update-slice_fusion.refs_0_), channel_id=1, source_target_pairs={{0,2},{1,3},{2,0},{3,1},{4,6},{5,7},{6,4},{7,5},{8,10},{9,11},{10,... | collective-permute-start | bytes 1474568 | tf_op jit(solution)/shard_map/ppermute | solution.py:50
  43.0 13.7 %collective-permute-start.8 = (bf16[1152,128]{1,0:T(8,128)(2,1)S(1)}, bf16[1152,128]{1,0:T(8,128)(2,1)S(1)}, u32[]{:S(2)}, u32[]{:S(2)}) collective-permute-start(bf16[1152,128]{1,0:T(8,128)(2,1)S(1)} %get-tuple-element.87), channel_id=1, source_target_pairs={{0,192},{64,0},{128,64},{192,128},{1,193},{65,1},{129,65},{193,129... | collective-permute-start | bytes 884744 | tf_op jit(solution)/shard_map/ppermute | solution.py:58
  45.8 14.3 %collective-permute-start.14 = (bf16[2,80,2048]{2,1,0:T(8,128)(2,1)}, bf16[2,80,2048]{2,1,0:T(8,128)(2,1)}, u32[]{:S(2)}, u32[]{:S(2)}) collective-permute-start(bf16[2,80,2048]{2,1,0:T(8,128)(2,1)} %local_slots.1.refs_8_), channel_id=1, source_target_pairs={{0,8},{8,0},{16,24},{24,16},{32,40},{40,32},{48,56},{56,48},{1,9},... | collective-permute-start | bytes 1966088 | tf_op jit(solution)/shard_map/ppermute | solution.py:29
  48.2 10.5 %collective-permute-start.13 = (bf16[960,256]{1,0:T(8,128)(2,1)}, bf16[960,256]{1,0:T(8,128)(2,1)}, u32[]{:S(2)}, u32[]{:S(2)}) collective-permute-start(bf16[960,256]{1,0:T(8,128)(2,1)} %collective-permute-done.9.refs_3_), channel_id=1, source_target_pairs={{0,8},{8,0},{16,24},{24,16},{32,40},{40,32},{48,56},{56,48},{1,9},... | collective-permute-start | bytes 1474568 | tf_op jit(solution)/shard_map/ppermute | solution.py:29
  56.2 2.9 %collective-permute-start.10 = (bf16[960,256]{1,0:T(8,128)(2,1)S(1)}, bf16[960,256]{1,0:T(8,128)(2,1)}, u32[]{:S(2)}, u32[]{:S(2)}) collective-permute-start(bf16[960,256]{1,0:T(8,128)(2,1)S(1)} %slice_dynamic-update-slice_fusion.refs_0_), channel_id=1, source_target_pairs={{0,8},{8,0},{16,24},{24,16},{32,40},{40,32},{48,56},{56,48},{1,9},... | collective-permute-start | bytes 1474568 | tf_op jit(solution)/shard_map/ppermute | solution.py:29
  56.2 3.2 %collective-permute-start.11 = (bf16[960,256]{1,0:T(8,128)(2,1)}, bf16[960,256]{1,0:T(8,128)(2,1)}, u32[]{:S(2)}, u32[]{:S(2)}) collective-permute-start(bf16[960,256]{1,0:T(8,128)(2,1)} %collective-permute-done.4.refs_1_), channel_id=1, source_target_pairs={{0,8},{8,0},{16,24},{24,16},{32,40},{40,32},{48,56},{56,48},{1,9},... | collective-permute-start | bytes 1474568 | tf_op jit(solution)/shard_map/ppermute | solution.py:29
  56.7 3.4 %collective-permute-start.12 = (bf16[960,256]{1,0:T(8,128)(2,1)}, bf16[960,256]{1,0:T(8,128)(2,1)}, u32[]{:S(2)}, u32[]{:S(2)}) collective-permute-start(bf16[960,256]{1,0:T(8,128)(2,1)} %collective-permute-done.7.refs_2_), channel_id=1, source_target_pairs={{0,8},{8,0},{16,24},{24,16},{32,40},{40,32},{48,56},{56,48},{1,9},... | collective-permute-start | bytes 1474568 | tf_op jit(solution)/shard_map/ppermute | solution.py:29
  72.5 3.3 %collective-permute-start.15 = (bf16[640,1024]{1,0:T(8,128)(2,1)}, bf16[640,1024]{1,0:T(8,128)(2,1)S(1)}, u32[]{:S(2)}, u32[]{:S(2)}) collective-permute-start(bf16[640,1024]{1,0:T(8,128)(2,1)} %get-tuple-element.104.grads), channel_id=1, source_target_pairs={{0,8},{8,0},{16,24},{24,16},{32,40},{40,32},{48,56},{56,48},{1,9},... | collective-permute-start | bytes 3932168 | tf_op jit(solution)/shard_map/ppermute | solution.py:29
  73.2 2.4 %collective-permute-start.16 = (f32[8,128]{1,0:T(8,128)S(1)}, f32[8,128]{1,0:T(8,128)S(1)}, u32[]{:S(2)}, u32[]{:S(2)}) collective-permute-start(f32[8,128]{1,0:T(8,128)S(1)} %pad.9.router_a), channel_id=1, source_target_pairs={{0,8},{8,0},{16,24},{24,16},{32,40},{40,32},{48,56},{56,48},{1,9},... | collective-permute-start | bytes 12296 | tf_op jit(solution)/shard_map/ppermute | solution.py:29
  80.4 12.5 %collective-permute-start.17 = (bf16[656,256]{1,0:T(8,128)(2,1)S(1)}, bf16[656,256]{1,0:T(8,128)(2,1)S(1)}, u32[]{:S(2)}, u32[]{:S(2)}) collective-permute-start(bf16[656,256]{1,0:T(8,128)(2,1)S(1)} %get-tuple-element.116), channel_id=1, source_target_pairs={{0,1},{1,2},{2,3},{3,0},{4,5},{5,6},{6,7},{7,4},{8,9},{9,10},{10,1... | collective-permute-start | bytes 1007624 | tf_op jit(solution)/shard_map/ppermute | solution.py:50
  80.5 12.4 %collective-permute-start.18 = (bf16[656,256]{1,0:T(8,128)(2,1)S(1)}, bf16[656,256]{1,0:T(8,128)(2,1)S(1)}, u32[]{:S(2)}, u32[]{:S(2)}) collective-permute-start(bf16[656,256]{1,0:T(8,128)(2,1)S(1)} %get-tuple-element.117), channel_id=1, source_target_pairs={{0,2},{1,3},{2,0},{3,1},{4,6},{5,7},{6,4},{7,5},{8,10},{9,11},{10,... | collective-permute-start | bytes 1007624 | tf_op jit(solution)/shard_map/ppermute | solution.py:50
  85.1 14.0 %collective-permute-start.19 = (bf16[656,256]{1,0:T(8,128)(2,1)S(1)}, bf16[656,256]{1,0:T(8,128)(2,1)S(1)}, u32[]{:S(2)}, u32[]{:S(2)}) collective-permute-start(bf16[656,256]{1,0:T(8,128)(2,1)S(1)} %get-tuple-element.118), channel_id=1, source_target_pairs={{0,3},{1,0},{2,1},{3,2},{4,7},{5,4},{6,5},{7,6},{8,11},{9,8},{10,9... | collective-permute-start | bytes 1007624 | tf_op jit(solution)/shard_map/ppermute | solution.py:50
  100.3 9.7 %collective-permute-start.20 = (bf16[176,256]{1,0:T(8,128)(2,1)S(1)}, bf16[176,256]{1,0:T(8,128)(2,1)S(1)}, u32[]{:S(2)}, u32[]{:S(2)}) collective-permute-start(bf16[176,256]{1,0:T(8,128)(2,1)S(1)} %get-tuple-element.124), channel_id=1, source_target_pairs={{0,192},{1,193},{2,194},{3,195},{4,196},{5,197},{6,198},{7,199},{8... | collective-permute-start | bytes 270344 | tf_op jit(solution)/shard_map/ppermute | solution.py:46
  103.1 6.9 %collective-permute-start.21 = (bf16[176,256]{1,0:T(8,128)(2,1)S(1)}, bf16[176,256]{1,0:T(8,128)(2,1)S(1)}, u32[]{:S(2)}, u32[]{:S(2)}) collective-permute-start(bf16[176,256]{1,0:T(8,128)(2,1)S(1)} %get-tuple-element.125), channel_id=1, source_target_pairs={{0,240},{1,241},{2,242},{3,243},{4,244},{5,245},{6,246},{7,247},{8... | collective-permute-start | bytes 270344 | tf_op jit(solution)/shard_map/ppermute | solution.py:46
  106.6 6.5 %collective-permute-start.23 = (bf16[176,256]{1,0:T(8,128)(2,1)S(1)}, bf16[176,256]{1,0:T(8,128)(2,1)S(1)}, u32[]{:S(2)}, u32[]{:S(2)}) collective-permute-start(bf16[176,256]{1,0:T(8,128)(2,1)S(1)} %get-tuple-element.127), channel_id=1, source_target_pairs={{0,208},{1,209},{2,210},{3,211},{4,212},{5,213},{6,214},{7,215},{8... | collective-permute-start | bytes 270344 | tf_op jit(solution)/shard_map/ppermute | solution.py:46
  106.6 9.5 %collective-permute-start.22 = (bf16[176,256]{1,0:T(8,128)(2,1)S(1)}, bf16[176,256]{1,0:T(8,128)(2,1)S(1)}, u32[]{:S(2)}, u32[]{:S(2)}) collective-permute-start(bf16[176,256]{1,0:T(8,128)(2,1)S(1)} %x_sum.2), channel_id=1, source_target_pairs={{0,228},{1,229},{2,230},{3,231},{4,224},{5,225},{6,226},{7,227},{8... | collective-permute-start | bytes 270344 | tf_op jit(solution)/shard_map/ppermute | solution.py:46
  116.4 4.0 %collective-permute-start.24 = (bf16[272,256]{1,0:T(8,128)(2,1)S(1)}, bf16[272,256]{1,0:T(8,128)(2,1)S(1)}, u32[]{:S(2)}, u32[]{:S(2)}) collective-permute-start(bf16[272,256]{1,0:T(8,128)(2,1)S(1)} %return_slots.1.partial), channel_id=1, source_target_pairs={{0,4},{1,5},{2,6},{3,7},{4,0},{5,1},{6,2},{7,3},{8,12},{9,13},{10,... | collective-permute-start | bytes 417800 | tf_op jit(solution)/shard_map/ppermute | solution.py:54
  121.0 4.1 %collective-permute-start.25 = (bf16[128,256]{1,0:T(8,128)(2,1)S(1)}, bf16[128,256]{1,0:T(8,128)(2,1)S(1)}, u32[]{:S(2)}, u32[]{:S(2)}) collective-permute-start(bf16[128,256]{1,0:T(8,128)(2,1)S(1)} %get-tuple-element.138), channel_id=1, source_target_pairs={{0,8},{8,0},{16,24},{24,16},{32,40},{40,32},{48,56},{56,48},{1,9},... | collective-permute-start | bytes 196616 | tf_op jit(solution)/shard_map/ppermute | solution.py:29
  124.2 3.7 %collective-permute-start.29 = (f32[8,128]{1,0:T(8,128)S(1)}, f32[8,128]{1,0:T(8,128)S(1)}, u32[]{:S(2)}, u32[]{:S(2)}) collective-permute-start(f32[8,128]{1,0:T(8,128)S(1)} %get-tuple-element.139), channel_id=1, source_target_pairs={{0,64},{64,128},{128,192},{192,0},{1,65},{65,129},{129,193},{193,1... | collective-permute-start | bytes 12296 | tf_op jit(solution)/shard_map/ppermute | solution.py:58
  125.2 4.8 %collective-permute-start.26 = (bf16[128,512]{1,0:T(8,128)(2,1)S(1)}, bf16[128,512]{1,0:T(8,128)(2,1)S(1)}, u32[]{:S(2)}, u32[]{:S(2)}) collective-permute-start(bf16[128,512]{1,0:T(8,128)(2,1)S(1)} %get-tuple-element.149), channel_id=1, source_target_pairs={{0,1},{1,2},{2,3},{3,0},{4,5},{5,6},{6,7},{7,4},{8,9},{9,10},{10,1... | collective-permute-start | bytes 393224 | tf_op jit(solution)/shard_map/ppermute | solution.py:50
  127.9 5.4 %collective-permute-start.27 = (bf16[128,512]{1,0:T(8,128)(2,1)S(1)}, bf16[128,512]{1,0:T(8,128)(2,1)S(1)}, u32[]{:S(2)}, u32[]{:S(2)}) collective-permute-start(bf16[128,512]{1,0:T(8,128)(2,1)S(1)} %get-tuple-element.149), channel_id=1, source_target_pairs={{0,2},{1,3},{2,0},{3,1},{4,6},{5,7},{6,4},{7,5},{8,10},{9,11},{10,... | collective-permute-start | bytes 393224 | tf_op jit(solution)/shard_map/ppermute | solution.py:50
  128.5 8.5 %collective-permute-start.28 = (bf16[128,512]{1,0:T(8,128)(2,1)S(1)}, bf16[128,512]{1,0:T(8,128)(2,1)S(1)}, u32[]{:S(2)}, u32[]{:S(2)}) collective-permute-start(bf16[128,512]{1,0:T(8,128)(2,1)S(1)} %get-tuple-element.149), channel_id=1, source_target_pairs={{0,3},{1,0},{2,1},{3,2},{4,7},{5,4},{6,5},{7,6},{8,11},{9,8},{10,9... | collective-permute-start | bytes 393224 | tf_op jit(solution)/shard_map/ppermute | solution.py:50
  (10 other events, 81.4 us)
